TPU v7x, 512 devices: a whole 4x8x8 slice. The times are simulated.
512 devices in a mesh: dp: 16 (over x, y_lo), mp: 32 (over y_hi, z, core).
Axes of the slice: x: 4, y: 8 (y_hi: 2, y_lo: 4; y = y_hi * 4 + y_lo), z: 8, core: 2. Of those that a mesh axis runs over, the one named last changes fastest.
Arguments:
- block_input: bfloat16 [2048, 6144], P('mp', 'dp'), may hold values from -64 to 64
- ln_gain: float32 [6144], P('dp'), may hold values from 0.5 to 1.5
- w_qkv: bfloat16 [6144, 12288], P('dp', 'mp'), may hold values from -0.078125 to 0.078125
- w_in: bfloat16 [6144, 12288], P('dp', 'mp'), may hold values from -0.078125 to 0.078125
- w_o: bfloat16 [4096, 6144], P('mp', 'dp'), may hold values from -0.09375 to 0.09375
- w_out: bfloat16 [12288, 6144], P('mp', 'dp'), may hold values from -0.0546875 to 0.0546875
- q_gain: float32 [32, 128], P('mp'), may hold values from 0.5 to 1.5
- k_gain: float32 [32, 128], P('mp'), may hold values from 0.5 to 1.5
- cotangent: bfloat16 [2048, 6144], P('mp', 'dp'), may hold values from -3 to 3
Outputs:
- output: bfloat16 [2048, 6144], P('mp', 'dp')
- grad_x: bfloat16 [2048, 6144], P('mp', 'dp')
- grad_w_qkv: bfloat16 [6144, 12288], P('dp', 'mp')
- grad_w_in: bfloat16 [6144, 12288], P('dp', 'mp')
- grad_w_o: bfloat16 [4096, 6144], P('mp', 'dp')
- grad_w_out: bfloat16 [12288, 6144], P('mp', 'dp')
All inputs are finite; a program needn't handle non-finite values.
Results may differ from a plain program's by a relative error of at most 0.038.
Values may be sent and summed in bfloat16 or wider, within the bound.
A program may use at most 64 MiB of HBM per device.

v0:
```python
import math

import jax
import jax.numpy as jnp
from jax import lax
from jax.sharding import PartitionSpec as P

D = 6144
PATCH = 128


epsilon = 1e-06


def row_totals(pieces):
    return lax.psum(pieces, "dp")


def token_rows(block):
    return lax.all_gather(block, "mp", axis=0, tiled=True)


def image_rows(block):
    return lax.all_gather(block, "dp", axis=0, tiled=True)


def feature_totals(left, product):
    return lax.psum_scatter(
        product(left).astype(jnp.bfloat16), "dp", scatter_dimension=0, tiled=True
    ).astype(jnp.float32)


def token_totals(left, product):
    return lax.psum_scatter(
        product(left).astype(jnp.bfloat16), "mp", scatter_dimension=0, tiled=True
    ).astype(jnp.float32)


def head_norm(values, gain):
    centre = values - jnp.mean(values, -1, keepdims=True)
    scaling = 1.0 / jnp.sqrt(jnp.mean(centre * centre, -1, keepdims=True) + epsilon)
    unit = centre * scaling
    return (unit * gain, unit, scaling)


def head_back(grad, unit, scaling, gain):
    local_grad = grad * gain
    return scaling * (
        local_grad
        - jnp.mean(local_grad, -1, keepdims=True)
        - unit * jnp.mean(local_grad * unit, -1, keepdims=True)
    )


def gelu_tanh(values):
    return jax.nn.gelu(values, approximate=True)


def shards(block_input, ln_gain, w_qkv, w_in, w_o, w_out, q_gain, k_gain, cotangent):
    heads_here = q_gain.shape[0]
    head_size = q_gain.shape[1]
    head_cols = heads_here * head_size
    factor = 1.0 / math.sqrt(head_size)
    contract_last = (((1,), (1,)), ((), ()))
    contract_first = (((0,), (0,)), ((), ()))
    inputs = block_input.astype(jnp.float32)
    mean = row_totals(jnp.sum(inputs, 1)) / D
    centred_raw = inputs - mean[:, None]
    spread = row_totals(jnp.sum(centred_raw * centred_raw, 1)) / D
    scaling = (1.0 / jnp.sqrt(spread + epsilon))[:, None]
    centred = centred_raw * scaling
    normed = (centred * ln_gain).astype(jnp.bfloat16)
    normed_all = token_rows(normed)
    both_weights = jnp.concatenate([w_qkv, w_in], 1)

    def project_in(rows):
        return jnp.dot(rows, both_weights, preferred_element_type=jnp.float32)

    features = feature_totals(normed_all, project_in)
    local_rows = features.shape[0]
    triples = features[:, : 3 * head_cols].reshape(local_rows, heads_here, 3, head_size)
    pre = features[:, 3 * head_cols :]
    queries, query_unit, query_scale = head_norm(triples[:, :, 0], q_gain)
    keys_normed, key_unit, key_scale = head_norm(triples[:, :, 1], k_gain)
    query_b = queries.astype(jnp.bfloat16)
    key_b = keys_normed.astype(jnp.bfloat16)
    value_b = triples[:, :, 2].astype(jnp.bfloat16)
    images_here = local_rows // PATCH
    query_img = query_b.reshape(images_here, PATCH, heads_here, head_size)
    key_img = key_b.reshape(images_here, PATCH, heads_here, head_size)
    value_img = value_b.reshape(images_here, PATCH, heads_here, head_size)
    scores = (
        jnp.einsum("iphd,iqhd->ihpq", query_img, key_img, preferred_element_type=jnp.float32)
        * factor
    )
    expo = jnp.exp(scores)
    prob = expo / jnp.sum(expo, -1, keepdims=True)
    prob_b = prob.astype(jnp.bfloat16)
    attended = jnp.einsum("ihpq,iqhd->iphd", prob_b, value_img, preferred_element_type=jnp.float32)
    attended = attended.astype(jnp.bfloat16).reshape(local_rows, head_cols)
    active = gelu_tanh(pre).astype(jnp.bfloat16)
    mixed = jnp.concatenate([attended, active], 1)
    mixed_all = image_rows(mixed)
    out_weights = jnp.concatenate([w_o, w_out], 0)

    def project_out(rows):
        return jnp.dot(rows, out_weights, preferred_element_type=jnp.float32)

    output = (inputs + token_totals(mixed_all, project_out)).astype(jnp.bfloat16)
    cotangent_all = token_rows(cotangent)
    out_grads = lax.dot_general(
        mixed_all, cotangent_all, contract_first, preferred_element_type=jnp.float32
    )
    grad_w_o = out_grads[:head_cols].astype(jnp.bfloat16)
    grad_w_out = out_grads[head_cols:].astype(jnp.bfloat16)

    def back_out(rows):
        return lax.dot_general(rows, out_weights, contract_last, preferred_element_type=jnp.float32)

    grad_mixed = feature_totals(cotangent_all, back_out)
    grad_attn = (
        grad_mixed[:, :head_cols]
        .astype(jnp.bfloat16)
        .reshape(images_here, PATCH, heads_here, head_size)
    )
    _, pullback = jax.vjp(gelu_tanh, pre)
    grad_pre = pullback(grad_mixed[:, head_cols:])[0].astype(jnp.bfloat16)
    dprob = jnp.einsum("iphd,iqhd->ihpq", grad_attn, value_img, preferred_element_type=jnp.float32)
    delta = jnp.sum(prob * dprob, -1, keepdims=True)
    dscore = (prob * (dprob - delta)).astype(jnp.bfloat16)
    grad_qn = (
        jnp.einsum("ihpq,iqhd->iphd", dscore, key_img, preferred_element_type=jnp.float32) * factor
    )
    key_part = jnp.einsum("ihpq,iphd->iqhd", dscore, query_img, preferred_element_type=jnp.float32)
    value_part = jnp.einsum(
        "ihpq,iphd->iqhd", prob_b, grad_attn, preferred_element_type=jnp.float32
    )
    grad_kn = key_part.reshape(local_rows, heads_here, head_size)
    grad_v = value_part.reshape(local_rows, heads_here, head_size)
    grad_q = head_back(
        grad_qn.reshape(local_rows, heads_here, head_size), query_unit, query_scale, q_gain
    )
    grad_k = head_back(grad_kn * factor, key_unit, key_scale, k_gain)
    grad_qkv = (
        jnp.stack([grad_q, grad_k, grad_v], 2)
        .reshape(local_rows, 3 * head_cols)
        .astype(jnp.bfloat16)
    )
    grads = jnp.concatenate([grad_qkv, grad_pre], 1)
    grads_all = image_rows(grads)
    weight_grads = lax.dot_general(
        normed_all, grads_all, contract_first, preferred_element_type=jnp.float32
    )
    grad_w_qkv = weight_grads[:, : 3 * head_cols].astype(jnp.bfloat16)
    grad_w_in = weight_grads[:, 3 * head_cols :].astype(jnp.bfloat16)

    def back_in(rows):
        return lax.dot_general(
            rows, both_weights, contract_last, preferred_element_type=jnp.float32
        )

    grad_normed = token_totals(grads_all, back_in)
    local_grad = grad_normed * ln_gain
    back_sums = row_totals((jnp.sum(local_grad, 1), jnp.sum(local_grad * centred, 1)))
    first = (back_sums[0] / D)[:, None]
    second = (back_sums[1] / D)[:, None]
    grad_x = (
        cotangent.astype(jnp.float32) + scaling * (local_grad - first - centred * second)
    ).astype(jnp.bfloat16)
    return (output, grad_x, grad_w_qkv, grad_w_in, grad_w_o, grad_w_out)


def solution(mesh):
    return jax.shard_map(
        shards,
        mesh=mesh,
        in_specs=(
            P("mp", "dp"),
            P("dp"),
            P("dp", "mp"),
            P("dp", "mp"),
            P("mp", "dp"),
            P("mp", "dp"),
            P("mp", None),
            P("mp", None),
            P("mp", "dp"),
        ),
        out_specs=(
            P("mp", "dp"),
            P("mp", "dp"),
            P("dp", "mp"),
            P("dp", "mp"),
            P("mp", "dp"),
            P("mp", "dp"),
        ),
        check_vma=False,
    )
```

profile of v0, /device:TPU:6, one launch (start us, length us, event | category | flops | bytes accessed | tf_op | source)
XLA Modules:
  0.0 922.0 jit_solution(6769535706858568915)
XLA Ops:
  7.2 0.0 all-gather.5.cloned.1.call-start
  7.2 0.9 convert_reduce_fusion
  8.1 37.0 %psum.28 = f32[64]{0:T(128)S(1)} all-reduce(f32[64]{0:T(128)S(1)} %convert_reduce_fusion), channel_id=1, replica_groups=mesh['dp'=16,'mp'=32] {'dp'}, use_global_device_ids=true, to_apply=%region_1.0 | all-reduce | flops 64 | bytes 512 | tf_op jit(solution)/shard_map/psum | solution.py:16
  45.1 1.0 fusion.25
  46.1 38.1 %psum.29 = f32[64]{0:T(128)S(1)} all-reduce(f32[64]{0:T(128)S(1)} %fusion.25), channel_id=1, replica_groups=mesh['dp'=16,'mp'=32] {'dp'}, use_global_device_ids=true, to_apply=%region_3.0 | all-reduce | flops 64 | bytes 512 | tf_op jit(solution)/shard_map/psum | solution.py:16
  84.3 1.5 fusion.19
  85.8 0.0 all-gather.5.cloned.1.call-update
  85.8 0.0 all-gather.9.cloned.1.call-start
  85.8 0.7 all-gather.9.cloned.1.call-update
  86.5 0.0 reduce-scatter.5.cloned.1.call-start
  86.6 1.0 constant_dynamic-update-slice_fusion.1
  87.6 1.0 constant_dynamic-update-slice_fusion
  88.6 92.5 %all-gather.5.cloned.1.call-done = bf16[2048,384]{1,0:T(8,128)(2,1)} async-done(((bf16[64,384]{1,0:T(8,128)(2,1)}), bf16[2048,384]{1,0:T(8,128)(2,1)}) %all-gather.5.cloned.1.call-update) | async-done | bytes 1572880 | tf_op jit(solution)/shard_map/all_gather | solution.py:20
  181.1 4.9 convolution_convert_fusion
  186.0 0.0 reduce-scatter.5.cloned.1.call-update
  186.0 0.0 reduce-scatter.9.cloned.1.call-start
  186.1 0.8 copy-done.5
  186.9 0.1 copy-done.3
  187.1 81.4 %all-gather.9.cloned.1.call-done = bf16[2048,384]{1,0:T(8,128)(2,1)} async-done(((bf16[64,384]{1,0:T(8,128)(2,1)}), bf16[2048,384]{1,0:T(8,128)(2,1)}) %all-gather.9.cloned.1.call-update) | async-done | bytes 1572880 | tf_op jit(solution)/shard_map/all_gather | solution.py:20
  268.4 4.1 fusion
  272.5 0.0 reduce-scatter.9.cloned.1.call-update
  272.5 0.0 all-gather.11.cloned.1.call-start
  272.6 85.7 %reduce-scatter.5.cloned.1.call-done = bf16[128,768]{1,0:T(8,128)(2,1)} async-done(((bf16[2048,768]{1,0:T(8,128)(2,1)}), bf16[128,768]{1,0:T(8,128)(2,1)}) %reduce-scatter.5.cloned.1.call-update) | async-done | bytes 196624 | tf_op jit(solution)/shard_map/reduce_scatter | solution.py:28
  358.3 1.0 slice.54
  359.3 0.1 copy.23
  359.5 0.1 copy.39
  359.6 0.1 copy.40
  359.7 0.2 multiply_reduce_fusion.4
  359.8 0.2 multiply_reduce_fusion.3
  360.1 0.3 fusion.54
  360.3 91.8 %reduce-scatter.9.cloned.1.call-done = bf16[128,512]{1,0:T(8,128)(2,1)} async-done(((bf16[2048,512]{1,0:T(8,128)(2,1)}), bf16[128,512]{1,0:T(8,128)(2,1)}) %reduce-scatter.9.cloned.1.call-update) | async-done | bytes 131088 | tf_op jit(solution)/shard_map/reduce_scatter | solution.py:28
  452.1 1.0 multiply_reduce_fusion.2
  453.2 0.3 fusion.36
  453.5 0.3 fusion.37
  453.9 0.1 fusion.31
  454.0 0.1 fusion.35
  454.2 0.9 fusion.3
  455.1 0.1 copy.32
  455.2 0.1 copy.33
  455.4 0.2 fusion.6
  455.6 0.7 pad_maximum_fusion
  456.3 0.0 all-gather.11.cloned.1.call-update
  456.3 0.0 all-gather.7.cloned.1.call-start
  456.4 0.2 fusion.2
  456.6 0.7 pad_maximum_fusion.1
  457.3 0.0 all-gather.7.cloned.1.call-update
  457.3 0.0 reduce-scatter.11.cloned.1.call-start
  457.3 92.7 %all-gather.11.cloned.1.call-done = bf16[2048,768]{1,0:T(8,128)(2,1)} async-done(((bf16[128,768]{1,0:T(8,128)(2,1)}), bf16[2048,768]{1,0:T(8,128)(2,1)}) %all-gather.11.cloned.1.call-update) | async-done | bytes 3145744 | tf_op jit(solution)/shard_map/all_gather | solution.py:24
  550.0 4.9 convolution_convert_fusion.2
  555.0 0.0 reduce-scatter.11.cloned.1.call-update
  555.0 0.0 reduce-scatter.7.cloned.1.call-start
  555.0 84.0 %all-gather.7.cloned.1.call-done = bf16[2048,512]{1,0:T(8,128)(2,1)} async-done(((bf16[128,512]{1,0:T(8,128)(2,1)}), bf16[2048,512]{1,0:T(8,128)(2,1)}) %all-gather.7.cloned.1.call-update) | async-done | bytes 2097168 | tf_op jit(solution)/shard_map/all_gather | solution.py:24
  639.1 4.0 convolution_convert_fusion.3
  643.1 0.0 reduce-scatter.7.cloned.1.call-update
  643.1 3.0 convolution_convert_fusion.5
  646.1 0.7 slice.63
  646.8 0.7 slice.64
  647.6 1.4 convolution_convert_fusion.4
  649.0 0.9 fusion.53
  649.9 132.0 %reduce-scatter.11.cloned.1.call-done = bf16[64,384]{1,0:T(8,128)(2,1)} async-done(((bf16[2048,384]{1,0:T(8,128)(2,1)}), bf16[64,384]{1,0:T(8,128)(2,1)}) %reduce-scatter.11.cloned.1.call-update) | async-done | bytes 49168 | tf_op jit(solution)/shard_map/reduce_scatter | solution.py:34
  781.8 1.0 fusion.27
  782.8 34.2 %all-reduce = (f32[64]{0:T(128)S(1)}, f32[64]{0:T(128)S(1)}) all-reduce(f32[64]{0:T(128)S(1)} %get-tuple-element.13, f32[64]{0:T(128)S(1)} %get-tuple-element.12), channel_id=1, replica_groups=mesh['dp'=16,'mp'=32] {'dp'}, use_global_device_ids=true, to_apply=%region_21.0 | all-reduce | flops 128 | bytes 1024 | tf_op jit(solution)/shard_map/psum | solution.py:16
  817.1 96.5 %reduce-scatter.7.cloned.1.call-done = bf16[64,384]{1,0:T(8,128)(2,1)} async-done(((bf16[2048,384]{1,0:T(8,128)(2,1)}), bf16[64,384]{1,0:T(8,128)(2,1)}) %reduce-scatter.7.cloned.1.call-update) | async-done | bytes 49168 | tf_op jit(solution)/shard_map/reduce_scatter | solution.py:34
  913.6 1.6 fusion.24
  (40 shorter events, 0.3 us)
Async XLA Ops:
  7.2 173.9 %all-gather.5.cloned.1.call-start = ((), (), s32[]{:S(2)}) async-start(), calls=%async_computation.4 | async-start | bytes 1622016 | tf_op jit(solution)/shard_map/all_gather | solution.py:20
  85.8 182.6 %all-gather.9.cloned.1.call-start = ((), (), s32[]{:S(2)}) async-start(), calls=%async_computation.8 | async-start | bytes 1622016 | tf_op jit(solution)/shard_map/all_gather | solution.py:20
  86.5 271.8 %reduce-scatter.5.cloned.1.call-start = ((), (), s32[]{:S(2)}) async-start(), calls=%async_computation.5 | async-start | bytes 3342336 | tf_op jit(solution)/shard_map/reduce_scatter | solution.py:28
  186.0 0.9 copy-start.5
  186.0 1.0 copy-start.3
  186.0 266.1 %reduce-scatter.9.cloned.1.call-start = ((), (), s32[]{:S(2)}) async-start(), calls=%async_computation.9 | async-start | bytes 2228224 | tf_op jit(solution)/shard_map/reduce_scatter | solution.py:28
  187.0 85.5 %copy-start.11 = (f32[1,128]{1,0:T(1,128)S(1)}, f32[1,128]{1,0:T(1,128)}, u32[]{:S(2)}) copy-start(f32[1,128]{1,0:T(1,128)} %param.16) | copy-start | bytes 1540
  272.5 87.6 %copy-start.8 = (f32[1,128]{1,0:T(1,128)S(1)}, f32[1,128]{1,0:T(1,128)}, u32[]{:S(2)}) copy-start(f32[1,128]{1,0:T(1,128)} %param.15) | copy-start | bytes 1540
  272.5 277.5 %all-gather.11.cloned.1.call-start = ((), (), s32[]{:S(2)}) async-start(), calls=%async_computation.10 | async-start | bytes 3342336 | tf_op jit(solution)/shard_map/all_gather | solution.py:24
  358.3 97.1 %copy-start.2 = (bf16[128,768]{1,0:T(8,128)(2,1)S(1)}, bf16[128,768]{1,0:T(8,128)(2,1)}, u32[]{:S(2)}) copy-start(bf16[128,768]{1,0:T(8,128)(2,1)} %reduce-scatter.5.cloned.1.call-done) | copy-start | bytes 589828
  452.1 3.3 copy-start.6
  456.3 182.8 %all-gather.7.cloned.1.call-start = ((), (), s32[]{:S(2)}) async-start(), calls=%async_computation.6 | async-start | bytes 2228224 | tf_op jit(solution)/shard_map/all_gather | solution.py:24
  457.3 324.6 %reduce-scatter.11.cloned.1.call-start = ((), (), s32[]{:S(2)}) async-start(), calls=%async_computation.11 | async-start | bytes 1622016 | tf_op jit(solution)/shard_map/reduce_scatter | solution.py:34
  555.0 88.1 %copy-start = (bf16[2048,384]{1,0:T(8,128)(2,1)S(1)}, bf16[2048,384]{1,0:T(8,128)(2,1)}, u32[]{:S(2)}) copy-start(bf16[2048,384]{1,0:T(8,128)(2,1)} %all-gather.9.cloned.1.call-done) | copy-start | bytes 4718596
  555.0 358.6 %reduce-scatter.7.cloned.1.call-start = ((), (), s32[]{:S(2)}) async-start(), calls=%async_computation.7 | async-start | bytes 1622016 | tf_op jit(solution)/shard_map/reduce_scatter | solution.py:34
  643.1 4.4 copy-start.9
  643.1 4.4 copy-start.10
  647.6 134.3 %copy-start.1 = (bf16[64,384]{1,0:T(8,128)(2,1)S(1)}, bf16[64,384]{1,0:T(8,128)(2,1)}, u32[]{:S(2)}) copy-start(bf16[64,384]{1,0:T(8,128)(2,1)} %param.9) | copy-start | bytes 147460
  647.6 134.3 %copy-start.7 = (f32[384]{0:T(512)S(1)}, f32[384]{0:T(512)}, u32[]{:S(2)}) copy-start(f32[384]{0:T(512)} %param.10) | copy-start | bytes 4612
  647.6 266.0 %copy-start.4 = (bf16[64,384]{1,0:T(8,128)(2,1)S(1)}, bf16[64,384]{1,0:T(8,128)(2,1)}, u32[]{:S(2)}) copy-start(bf16[64,384]{1,0:T(8,128)(2,1)} %param.17) | copy-start | bytes 147460
Sparse Core Ops, SparseCore 0:
  85.9 95.1 all-gather.4
  184.5 83.9 all-gather.8
  271.3 86.9 reduce-scatter.4
  361.0 91.0 reduce-scatter.8
  456.4 93.5 all-gather.10
  552.5 86.5 all-gather.6
  643.8 138.0 reduce-scatter.10
  786.5 127.0 reduce-scatter.6
where the time goes:
time: 923 us; the launch traced here: 922 us
  waiting for transfers between devices  757 us (82%)
  blocking collectives  109 us (12%)
  matrix products  25.4 us (3%)
  between operations  14.4 us (2%)
    reduce_scatter x2, waiting for transfers between devices, token_totals(): lax.psum_scatter(product(left).astype(jnp.bfloat16), 'mp', scatter_dimens...  228 us
    reduce_scatter x2, waiting for transfers between devices, feature_totals(): lax.psum_scatter(product(left).astype(jnp.bfloat16), 'dp', scatter_dimens...  177 us
    all_gather x2, waiting for transfers between devices, image_rows(): return lax.all_gather(block, 'dp', axis=0, tiled=True)  177 us
    all_gather x2, waiting for transfers between devices, token_rows(): return lax.all_gather(block, 'mp', axis=0, tiled=True)  174 us
    psum x3, blocking collectives, row_totals(): return lax.psum(pieces, 'dp')  109 us
  transfers between devices with their start and end apart: 8, of which 8 were waited for; matrix products, arithmetic and copies ran while one was open for 3% of the time, Pallas kernels for 0%

commit v1 on v0

v1 whole, which is shorter than its diff:
```python
import math

import jax
import jax.numpy as jnp
from jax import lax
from jax.experimental import pallas as pl
from jax.experimental.pallas import tpu as pltpu
from jax.sharding import PartitionSpec as P

MESH = pl.DeviceIdType.MESH
D = 6144
FEATURES = 384
N_DP = 16
epsilon = 1e-06
F32 = jnp.float32
BF16 = jnp.bfloat16
FACTOR = 1.0 / math.sqrt(128)
GELU_ROOT = 0.7978845608028654
GELU_CUBE = 0.044715
NT = (((1,), (1,)), ((), ()))
TN = (((0,), (0,)), ((), ()))
COPIES = 200


def mm(a, b):
    return jnp.dot(a, b, preferred_element_type=F32)


def mm_nt(a, b):
    return lax.dot_general(a, b, NT, preferred_element_type=F32)


def mm_tn(a, b):
    return lax.dot_general(a, b, TN, preferred_element_type=F32)


def up(v):
    return v.astype(F32)


def head_norm(values, gain):
    centre = values - jnp.mean(values, -1, keepdims=True)
    scaling = 1.0 / jnp.sqrt(jnp.mean(centre * centre, -1, keepdims=True) + epsilon)
    unit = centre * scaling
    return (unit * gain, unit, scaling)


def head_back(grad, unit, scaling, gain):
    local_grad = grad * gain
    return scaling * (
        local_grad
        - jnp.mean(local_grad, -1, keepdims=True)
        - unit * jnp.mean(local_grad * unit, -1, keepdims=True)
    )


def columns_to_rows(first, second):
    lane = lax.broadcasted_iota(jnp.int32, (64, 128), 1)
    block = jnp.where(lane == 0, first, jnp.where(lane == 1, second, 0.0))
    block = jnp.concatenate([block, jnp.zeros((64, 128), F32)], 0)
    return block.T[:8]


def rows_to_columns(first, second):
    row = lax.broadcasted_iota(jnp.int32, (128, 128), 0)
    block = jnp.where(row == 0, first, jnp.where(row == 1, second, 0.0)).T
    return block[:64, 0:1], block[:64, 1:2]


def kernel(
    x_ref, cot_ref, gain_ref, wqkv_ref, win_ref, wo_ref, wout_ref, qg_ref, kg_ref,
    out_ref, gx_ref, gwqkv_ref, gwin_ref, gwo_ref, gwout_ref,
    cot_all, nrm_all, bw, ow, stats, stats_b, cen_ref, scl_ref,
    g1, g2, fp, rg1, rg2, rfp, s1, s2, sf, tg1, tg2, tfp,
    m_all, ra_all, rb_all, eo, eg, reo, reg, so, sg, lo, ro, lg, rg, fo, fg, yo, yg, ryo, ryg,
    send, recv,
):
    d = lax.axis_index("dp")
    m = lax.axis_index("mp")
    x, y = d // 4, lax.rem(d, 4)
    h, z, c = m // 16, lax.rem(m // 2, 8), lax.rem(m, 2)

    def dp_at(xx, yy):
        return (xx * 4 + yy, m)

    x_peers = [dp_at(lax.rem(x + o, 4), y) for o in (1, 2, 3)]
    y_peers = [dp_at(x, lax.rem(y + o, 4)) for o in (1, 2, 3)]
    dp_peers = [(lax.rem(d + o, N_DP), m) for o in range(1, N_DP)]
    hi_peer = (d, (1 - h) * 16 + z * 2 + c)
    z_right = (d, h * 16 + lax.rem(z + 1, 8) * 2 + c)
    z_left = (d, h * 16 + lax.rem(z + 7, 8) * 2 + c)
    core_peer = (d, m + 1 - 2 * c)

    barrier = pltpu.get_barrier_semaphore()
    everyone = dp_peers + [hi_peer, z_right, z_left, core_peer]
    for peer in everyone:
        pl.semaphore_signal(barrier, inc=1, device_id=peer, device_id_type=MESH)

    started = []

    def push(src, dst, peer):
        n = len(started)
        copy = pltpu.make_async_remote_copy(
            src_ref=src, dst_ref=dst, send_sem=send.at[n], recv_sem=recv.at[n],
            device_id=peer, device_id_type=MESH,
        )
        copy.start()
        started.append(copy)
        return copy

    def arrive(copies):
        for copy in copies:
            copy.wait_recv()

    mine = h * 8 + z
    cot_all[mine, c] = cot_ref[...]
    inputs = up(x_ref[...])
    local_mean = jnp.sum(inputs, 1, keepdims=True) / FEATURES
    local_centre = inputs - local_mean
    local_m2 = jnp.sum(local_centre * local_centre, 1, keepdims=True)
    stats[d] = columns_to_rows(local_mean, local_m2)
    bw[:, :384] = wqkv_ref[...]
    bw[:, 384:] = win_ref[...]
    ow[:128] = wo_ref[...]
    ow[128:] = wout_ref[...]
    pl.semaphore_wait(barrier, len(everyone))

    def hi_start(a):
        return [push(a.at[mine, c], a.at[mine, c], hi_peer)]

    def ring_start(a, kind, s):
        hh = h if kind == 0 else 1 - h
        right = hh * 8 + lax.rem(z + 9 - s, 8)
        left = hh * 8 + lax.rem(z + s - 1, 8)
        if s == 4:
            first, second = pl.ds(0, 32), pl.ds(32, 32)
            return [
                push(a.at[right, c, first], a.at[right, c, first], z_right),
                push(a.at[left, c, second], a.at[left, c, second], z_left),
            ]
        return [
            push(a.at[right, c], a.at[right, c], z_right),
            push(a.at[left, c], a.at[left, c], z_left),
        ]

    def core_start(a):
        return [push(a.at[:, c], a.at[:, c], core_peer)]

    ch = hi_start(cot_all)
    ca = ring_start(cot_all, 0, 1)
    st = [push(stats.at[d], stats.at[d], peer) for peer in dp_peers]
    arrive(ch)
    cb = ring_start(cot_all, 1, 1)
    arrive(ca)
    ca = ring_start(cot_all, 0, 2)
    arrive(st)
    every = stats[...]
    mean_row = jnp.sum(every[:, 0:1, :], 0) / N_DP
    apart = every[:, 0:1, :] - mean_row[None]
    m2_row = jnp.sum(every[:, 1:2, :], 0) + FEATURES * jnp.sum(apart * apart, 0)
    scaling_row = 1.0 / jnp.sqrt(m2_row / D + epsilon)
    mean, scaling = rows_to_columns(mean_row, scaling_row)
    centred = (inputs - mean) * scaling
    cen_ref[...] = centred
    scl_ref[...] = jnp.broadcast_to(scaling, (64, 128))
    nrm_all[mine, c] = (centred * gain_ref[...]).astype(BF16)
    nh = hi_start(nrm_all)
    na = ring_start(nrm_all, 0, 1)
    arrive(cb)
    cb = ring_start(cot_all, 1, 2)
    arrive(ca)
    ca = ring_start(cot_all, 0, 3)
    arrive(nh)
    nb = ring_start(nrm_all, 1, 1)
    arrive(na)
    na = ring_start(nrm_all, 0, 2)
    arrive(cb)
    cb = ring_start(cot_all, 1, 3)
    arrive(ca)
    ca = ring_start(cot_all, 0, 4)
    arrive(nb)
    nb = ring_start(nrm_all, 1, 2)
    arrive(na)
    na = ring_start(nrm_all, 0, 3)
    arrive(cb)
    cb = ring_start(cot_all, 1, 4)
    arrive(ca)
    arrive(cb)
    cc = core_start(cot_all)
    arrive(nb)
    nb = ring_start(nrm_all, 1, 3)
    arrive(na)
    na = ring_start(nrm_all, 0, 4)
    arrive(cc)

    for xx in range(4):
        rows = cot_all[4 * xx : 4 * xx + 4].reshape(512, FEATURES)
        product = mm_nt(rows, ow[...]).astype(BF16)
        g1[xx] = product[:, :256].reshape(4, 128, 256)
        g2[xx] = product[:, 256:].reshape(4, 128, 256)
    w1 = [
        push(g1.at[:, lax.rem(y + o, 4)], rg1.at[o - 1], y_peers[o - 1]) for o in (1, 2, 3)
    ]
    w2 = [push(g2.at[lax.rem(x + o, 4)], rg2.at[o - 1], x_peers[o - 1]) for o in (1, 2, 3)]
    arrive(nb)
    nb = ring_start(nrm_all, 1, 4)
    arrive(na)
    arrive(nb)
    arrive(core_start(nrm_all))

    wf = [[], [], [], []]
    for o in (1, 2, 3, 0):
        xx = lax.rem(x + o, 4)
        rows = nrm_all[pl.ds(4 * xx, 4)].reshape(512, FEATURES)
        fp[xx] = mm(rows, bw[...]).astype(BF16).reshape(4, 128, 768)
        if o:
            for k in range(4):
                yy = lax.rem(y + k + 1, 4)
                wf[k].append(push(fp.at[xx, yy], rfp.at[o - 1, k], x_peers[o - 1]))

    def fsum(k):
        yy = lax.rem(y + k + 1, 4)
        return up(fp[x, yy]) + up(rfp[0, k]) + up(rfp[1, k]) + up(rfp[2, k])

    tf = []
    t2 = []
    for k in range(3):
        arrive(wf[k])
        sf[k] = fsum(k).astype(BF16)
        tf.append(push(sf.at[k], tfp.at[k], y_peers[k]))
        if k == 0:
            arrive(w2)
            for j in range(3):
                yy = lax.rem(y + j + 1, 4)
                total = up(g2[x, yy]) + up(rg2[0, yy]) + up(rg2[1, yy]) + up(rg2[2, yy])
                s2[j] = total.astype(BF16)
                t2.append(push(s2.at[j], tg2.at[j], y_peers[j]))
    arrive(w1)
    t1 = []
    for j in range(3):
        xx = lax.rem(x + j + 1, 4)
        total = up(g1[xx, y]) + up(rg1[0, xx]) + up(rg1[1, xx]) + up(rg1[2, xx])
        s1[j] = total.astype(BF16)
        t1.append(push(s1.at[j], tg1.at[j], x_peers[j]))
    arrive(t2)
    gm2 = up(g2[x, y]) + up(rg2[0, y]) + up(rg2[1, y]) + up(rg2[2, y])
    gm2 = gm2 + up(tg2[0]) + up(tg2[1]) + up(tg2[2])
    arrive(wf[3])
    own_sum = fsum(3)
    arrive(tf)
    features = own_sum + up(tfp[0]) + up(tfp[1]) + up(tfp[2])
    arrive(t1)
    gm1 = up(g1[x, y]) + up(rg1[0, x]) + up(rg1[1, x]) + up(rg1[2, x])
    gm1 = gm1 + up(tg1[0]) + up(tg1[1]) + up(tg1[2])

    qg, kg = qg_ref[...], kg_ref[...]
    queries, query_unit, query_scale = head_norm(features[:, :128], qg)
    keys, key_unit, key_scale = head_norm(features[:, 128:256], kg)
    query_b, key_b = queries.astype(BF16), keys.astype(BF16)
    value_b = features[:, 256:384].astype(BF16)
    pre = features[:, 384:]
    expo = jnp.exp(mm_nt(query_b, key_b) * FACTOR)
    prob = expo / jnp.sum(expo, -1, keepdims=True)
    prob_b = prob.astype(BF16)
    inner = GELU_ROOT * (pre + GELU_CUBE * (pre * pre * pre))
    bend = jnp.tanh(inner)
    m_all[x, y, :, :128] = mm(prob_b, value_b).astype(BF16)
    m_all[x, y, :, 128:] = (0.5 * pre * (1.0 + bend)).astype(BF16)
    own_m = m_all.at[x, y]
    m_y = [push(own_m, own_m, peer) for peer in y_peers]
    m_x = [push(own_m, own_m, peer) for peer in x_peers]
    slope = 0.5 * (1.0 + bend) + 0.5 * pre * (1.0 - bend * bend) * (
        GELU_ROOT * (1.0 + 3.0 * GELU_CUBE * (pre * pre))
    )
    grad_attn = gm1[:, :128].astype(BF16)
    grad_act = jnp.concatenate([gm1[:, 128:], gm2], 1)
    rb_all[x, y, :, 128:] = (grad_act * slope).astype(BF16)
    dprob = mm_nt(grad_attn, value_b)
    delta = jnp.sum(prob * dprob, -1, keepdims=True)
    dscore = (prob * (dprob - delta)).astype(BF16)
    grad_qn = mm(dscore, key_b) * FACTOR
    grad_kn = mm_tn(dscore, query_b) * FACTOR
    ra_all[x, y, :, :128] = head_back(grad_qn, query_unit, query_scale, qg).astype(BF16)
    ra_all[x, y, :, 128:] = head_back(grad_kn, key_unit, key_scale, kg).astype(BF16)
    rb_all[x, y, :, :128] = mm_tn(prob_b, grad_attn).astype(BF16)

    own_a, own_b = ra_all.at[x, y], rb_all.at[x, y]
    a_x = [push(own_a, own_a, peer) for peer in x_peers]
    b_y = [push(own_b, own_b, peer) for peer in y_peers]
    b_x = [push(own_b, own_b, peer) for peer in x_peers]
    for o in (1, 2, 3):
        arrive([m_y[o - 1]])
        block = m_all.at[x, lax.rem(y + 4 - o, 4)]
        m_x += [push(block, block, peer) for peer in x_peers]
    arrive(a_x)
    a_y = [push(ra_all.at[:, y], ra_all.at[:, y], peer) for peer in y_peers]
    for o in (1, 2, 3):
        arrive([b_y[o - 1]])
        block = rb_all.at[x, lax.rem(y + 4 - o, 4)]
        b_x += [push(block, block, peer) for peer in x_peers]

    def core_sum(e, r, s):
        own = e[:, pl.ds(c, 1)].reshape(16, 64, FEATURES)
        s[...] = (up(own) + up(r[...])).astype(BF16).reshape(2, 8, 64, FEATURES)

    def scatter_start(s_ref, l_ref, r_ref, s):
        right = lax.rem(z + 5 - s, 8)
        left = lax.rem(z + 3 + s, 8)
        if s == 1:
            first, second = pl.ds(0, 32), pl.ds(32, 32)
            return [
                push(s_ref.at[:, right, first], l_ref.at[0, :, first], z_right),
                push(s_ref.at[:, left, second], r_ref.at[0, :, second], z_left),
            ]
        return [
            push(s_ref.at[:, right], l_ref.at[s - 1], z_right),
            push(s_ref.at[:, left], r_ref.at[s - 1], z_left),
        ]

    def scatter_add(s_ref, l_ref, r_ref, s):
        right = lax.rem(z + 5 - s, 8)
        left = lax.rem(z + 3 + s, 8)
        if s == 2:
            first, second = pl.ds(0, 32), pl.ds(32, 32)
        else:
            first = second = pl.ds(0, 64)
        for at, rows, got in ((right, first, l_ref), (left, second, r_ref)):
            size = 32 if s == 2 else 64
            old = s_ref[:, pl.ds(at, 1), rows].reshape(2, size, FEATURES)
            new = (up(old) + up(got[s - 2, :, rows])).astype(BF16)
            s_ref[:, pl.ds(at, 1), rows] = new.reshape(2, 1, size, FEATURES)

    def scatter_last(s_ref, l_ref, r_ref, f_ref, y_ref, got_ref):
        own = s_ref[:, pl.ds(z, 1)].reshape(2, 64, FEATURES)
        f_ref[...] = up(own) + up(l_ref[3]) + up(r_ref[3])
        y_ref[...] = f_ref[1 - h].astype(BF16)
        return [push(y_ref, got_ref, hi_peer)]

    arrive(m_x)
    for xx in range(4):
        part = mm(m_all[xx].reshape(512, 512), ow[...])
        eo[4 * xx : 4 * xx + 4] = part.astype(BF16).reshape(4, 2, 64, FEATURES)
    ec = [push(eo.at[:, 1 - c], reo, core_peer)]
    arrive(ec)
    core_sum(eo, reo, so)
    ring = scatter_start(so, lo, ro, 1)
    grad_out = mm_tn(m_all[...].reshape(2048, 512), cot_all[...].reshape(2048, FEATURES))
    gwo_ref[...] = grad_out[:128].astype(BF16)
    gwout_ref[...] = grad_out[128:].astype(BF16)
    for s in (2, 3, 4):
        arrive(ring)
        scatter_add(so, lo, ro, s)
        ring = scatter_start(so, lo, ro, s)

    arrive(a_y)
    arrive(b_x)
    for xx in range(4):
        part = mm_nt(ra_all[xx].reshape(512, 256), bw[:, :256])
        part = part + mm_nt(rb_all[xx].reshape(512, 512), bw[:, 256:])
        eg[4 * xx : 4 * xx + 4] = part.astype(BF16).reshape(4, 2, 64, FEATURES)
    ec = [push(eg.at[:, 1 - c], reg, core_peer)]
    arrive(ring)
    yh = scatter_last(so, lo, ro, fo, yo, ryo)
    arrive(ec)
    core_sum(eg, reg, sg)
    ring = scatter_start(sg, lg, rg, 1)
    normed_t = nrm_all[...].reshape(2048, FEATURES)
    part = mm_tn(normed_t, ra_all[...].reshape(2048, 256))
    gwqkv_ref[:, :256] = part.astype(BF16)
    arrive(ring)
    scatter_add(sg, lg, rg, 2)
    ring = scatter_start(sg, lg, rg, 2)
    part = mm_tn(normed_t, rb_all[...].reshape(2048, 512))
    gwqkv_ref[:, 256:] = part[:, :128].astype(BF16)
    gwin_ref[...] = part[:, 128:].astype(BF16)
    for s in (3, 4):
        arrive(ring)
        scatter_add(sg, lg, rg, s)
        ring = scatter_start(sg, lg, rg, s)
    arrive(yh)
    out_ref[...] = (up(x_ref[...]) + fo[h] + up(ryo[...])).astype(BF16)
    arrive(ring)
    yh = scatter_last(sg, lg, rg, fg, yg, ryg)
    arrive(yh)
    local_grad = (fg[h] + up(ryg[...])) * gain_ref[...]
    centred = cen_ref[...]
    stats_b[d] = columns_to_rows(
        jnp.sum(local_grad, 1, keepdims=True),
        jnp.sum(local_grad * centred, 1, keepdims=True),
    )
    arrive([push(stats_b.at[d], stats_b.at[d], peer) for peer in dp_peers])
    sums = jnp.sum(stats_b[...], 0) / D
    first, second = rows_to_columns(sums[0:1], sums[1:2])
    scaling = scl_ref[...][:, 0:1]
    gx_ref[...] = (
        up(cot_ref[...]) + scaling * (local_grad - first - centred * second)
    ).astype(BF16)
    for copy in started:
        copy.wait_send()


def shards(block_input, ln_gain, w_qkv, w_in, w_o, w_out, q_gain, k_gain, cotangent):
    def vmem(*shape):
        return pltpu.VMEM(shape, BF16)

    scratch = [
        vmem(16, 2, 64, 384), vmem(16, 2, 64, 384), vmem(384, 768), vmem(512, 384),
        pltpu.VMEM((16, 8, 128), F32), pltpu.VMEM((16, 8, 128), F32),
        pltpu.VMEM((64, 384), F32), pltpu.VMEM((64, 128), F32),
        vmem(4, 4, 128, 256), vmem(4, 4, 128, 256), vmem(4, 4, 128, 768),
        vmem(3, 4, 128, 256), vmem(3, 4, 128, 256), vmem(3, 4, 128, 768),
        vmem(3, 128, 256), vmem(3, 128, 256), vmem(3, 128, 768),
        vmem(3, 128, 256), vmem(3, 128, 256), vmem(3, 128, 768),
        vmem(4, 4, 128, 512), vmem(4, 4, 128, 256), vmem(4, 4, 128, 512),
        vmem(16, 2, 64, 384), vmem(16, 2, 64, 384), vmem(16, 64, 384), vmem(16, 64, 384),
        vmem(2, 8, 64, 384), vmem(2, 8, 64, 384),
        vmem(4, 2, 64, 384), vmem(4, 2, 64, 384), vmem(4, 2, 64, 384), vmem(4, 2, 64, 384),
        pltpu.VMEM((2, 64, 384), F32), pltpu.VMEM((2, 64, 384), F32),
        vmem(64, 384), vmem(64, 384), vmem(64, 384), vmem(64, 384),
        pltpu.SemaphoreType.DMA((COPIES,)), pltpu.SemaphoreType.DMA((COPIES,)),
    ]
    args = (
        block_input, cotangent, ln_gain.reshape(1, -1), w_qkv, w_in, w_o, w_out, q_gain, k_gain,
    )
    outs = (block_input, cotangent, w_qkv, w_in, w_o, w_out)
    return pl.pallas_call(
        kernel,
        out_shape=tuple(jax.ShapeDtypeStruct(a.shape, BF16) for a in outs),
        in_specs=[pl.BlockSpec(memory_space=pltpu.VMEM)] * len(args),
        out_specs=tuple(pl.BlockSpec(memory_space=pltpu.VMEM) for _ in outs),
        scratch_shapes=scratch,
        compiler_params=pltpu.CompilerParams(
            collective_id=1, has_side_effects=True, vmem_limit_bytes=56 * 2**20
        ),
        name="block",
    )(*args)


def solution(mesh):
    return jax.shard_map(
        shards,
        mesh=mesh,
        in_specs=(
            P("mp", "dp"),
            P("dp"),
            P("dp", "mp"),
            P("dp", "mp"),
            P("mp", "dp"),
            P("mp", "dp"),
            P("mp", None),
            P("mp", None),
            P("mp", "dp"),
        ),
        out_specs=(
            P("mp", "dp"),
            P("mp", "dp"),
            P("dp", "mp"),
            P("dp", "mp"),
            P("mp", "dp"),
            P("mp", "dp"),
        ),
        check_vma=False,
    )
```

time: 923 us -> 196 us (0.21)
  waiting for transfers between devices: 757 us -> 0 us
  Pallas kernels: 0 us -> 188 us
  blocking collectives: 109 us -> 0 us
  matrix products: 25.4 us -> 0 us
  between operations: 14.4 us -> 0.65 us
    reduce_scatter x4 -> x0, waiting for transfers between devices: 406 us -> none  [the longest x2 228 us: token_totals(): lax.psum_scatter(product(left).astype(jnp.bfloat16), 'mp', scatter_dimens...]
    all_gather x4 -> x0, waiting for transfers between devices: 351 us -> none  [the longest x2 177 us: image_rows(): return lax.all_gather(block, 'dp', axis=0, tiled=True)]
    pallas_call x0 -> x1, Pallas kernels: none -> 188 us  [shards(): pl.pallas_call(kernel, out_shape=tuple((jax.ShapeDtypeStruct(a.shape, BF1...]
    psum x3 -> x0, blocking collectives: 109 us -> none  [row_totals(): return lax.psum(pieces, 'dp')]
    dot_general x12 -> x0, matrix products: 25.4 us -> none  [the longest x1 4.95 us: back_in(): lax.dot_general(rows, both_weights, contract_last, preferred_element_type...]
  transfers between devices with their start and end apart: 8 -> 0, of which waited for: 8 -> 0; matrix products, arithmetic and copies ran while one was open for 3% -> 0% of each run, Pallas kernels for 0% -> 0%
where the time goes in v1:
time: 196 us
  Pallas kernels  188 us (96%)
  local copies, waits for them, and re-layouts  7.38 us (4%)
    pallas_call x1, Pallas kernels, shards(): pl.pallas_call(kernel, out_shape=tuple((jax.ShapeDtypeStruct(a.shape, BF1...  188 us
    unnamed x14, local copies, waits for them, and re-layouts  6.13 us

profile of v1, /device:TPU:6, one launch (start us, length us, event | category | flops | bytes accessed | tf_op | source)
XLA Modules:
  0.0 195.6 jit_solution(7283128170729921517)
XLA Ops:
  0.6 1.2 reshape.15.gain_ref
  1.9 187.5 %block.1 = (bf16[64,384]{1,0:T(8,128)(2,1)}, bf16[64,384]{1,0:T(8,128)(2,1)}, bf16[384,384]{1,0:T(8,128)(2,1)}, bf16[384,384]{1,0:T(8,128)(2,1)}, bf16[128,384]{1,0:T(8,128)(2,1)}, /*index=5*/bf16[384,384]{1,0:T(8,128)(2,1)}) custom-call(bf16[64,384]{1,0:T(8,128)(2,1)} %x_ref.1, bf16[64,384]{1,0:T(8,128)(2,1)} %cot_ref.1, f32[1,384]{1,0:T(1,128)} %reshape.15.gain_ref, ...), custom_call_target="tpu_custom_call" | custom-call | tf_op jit(solution)/shard_map/block/pallas_call | solution.py:426
  189.4 0.0 copy-start.3
  189.4 1.4 copy.21
  190.9 0.0 copy-done.3
  190.9 0.6 copy.22
  191.5 0.0 copy-start.1
  191.5 1.7 copy.23
  193.2 0.0 copy-done.1
  193.3 0.0 copy-start.2
  193.3 0.0 copy-start
  193.3 0.7 copy.24
  194.0 0.2 copy-done.2
  194.2 0.6 copy.25
  194.9 0.0 copy-done
  194.9 0.7 copy.26
Async XLA Ops:
  189.4 1.4 copy-start.3
  191.5 1.8 copy-start.1
  193.3 1.0 copy-start.2
  193.3 1.6 copy-start

commit v2 on v1

v2 whole, which is shorter than its diff:
```python
import math

import jax
import jax.numpy as jnp
from jax import lax
from jax.experimental import pallas as pl
from jax.experimental.pallas import tpu as pltpu
from jax.sharding import PartitionSpec as P

MESH = pl.DeviceIdType.MESH
D = 6144
FEATURES = 384
N_DP = 16
epsilon = 1e-06
F32 = jnp.float32
BF16 = jnp.bfloat16
FACTOR = 1.0 / math.sqrt(128)
GELU_ROOT = 0.7978845608028654
GELU_CUBE = 0.044715
NT = (((1,), (1,)), ((), ()))
TN = (((0,), (0,)), ((), ()))
COPIES = 300
GATHER_ORDER = (0, 3, 1, 2)
SCATTER_ORDER = (2, 1, 3, 0)


def mm(a, b):
    return jnp.dot(a, b, preferred_element_type=F32)


def mm_nt(a, b):
    return lax.dot_general(a, b, NT, preferred_element_type=F32)


def mm_tn(a, b):
    return lax.dot_general(a, b, TN, preferred_element_type=F32)


def up(v):
    return v.astype(F32)


def head_norm(values, gain):
    centre = values - jnp.mean(values, -1, keepdims=True)
    scaling = 1.0 / jnp.sqrt(jnp.mean(centre * centre, -1, keepdims=True) + epsilon)
    unit = centre * scaling
    return (unit * gain, unit, scaling)


def head_back(grad, unit, scaling, gain):
    local_grad = grad * gain
    return scaling * (
        local_grad
        - jnp.mean(local_grad, -1, keepdims=True)
        - unit * jnp.mean(local_grad * unit, -1, keepdims=True)
    )


def columns_to_rows(first, second):
    lane = lax.broadcasted_iota(jnp.int32, (64, 128), 1)
    block = jnp.where(lane == 0, first, jnp.where(lane == 1, second, 0.0))
    block = jnp.concatenate([block, jnp.zeros((64, 128), F32)], 0)
    return block.T[:8]


def rows_to_columns(first, second):
    row = lax.broadcasted_iota(jnp.int32, (128, 128), 0)
    block = jnp.where(row == 0, first, jnp.where(row == 1, second, 0.0)).T
    return block[:64, 0:1], block[:64, 1:2]


def kernel(
    x_ref, cot_ref, gain_ref, wqkv_ref, win_ref, wo_ref, wout_ref, qg_ref, kg_ref,
    out_ref, gx_ref, gwqkv_ref, gwin_ref, gwo_ref, gwout_ref,
    cot_all, nrm_all, bw, ow, stats, stats_b, cen_ref, scl_ref,
    g1, rg1, s1, tg1,
    g2, hl2, hr2, fl2, fr2, s2, t2,
    fp, hlf, hrf, flf, frf, sf, tf,
    m_all, ra_all, rb_all, eo, eg, reo, reg, so, sg, lo, ro, lg, rg, fo, fg, yo, yg, ryo, ryg,
    send, recv,
):
    d = lax.axis_index("dp")
    m = lax.axis_index("mp")
    x, y = d // 4, lax.rem(d, 4)
    h, z, c = m // 16, lax.rem(m // 2, 8), lax.rem(m, 2)

    def dp_at(xx, yy):
        return (xx * 4 + yy, m)

    def around(v, o):
        return lax.rem(v + o, 4)

    x_peers = [dp_at(around(x, o), y) for o in (1, 2, 3)]
    y_peers = [dp_at(x, around(y, o)) for o in (1, 2, 3)]
    x_right, x_left = x_peers[0], x_peers[2]
    hi_peer = (d, (1 - h) * 16 + z * 2 + c)
    z_right = (d, h * 16 + lax.rem(z + 1, 8) * 2 + c)
    z_left = (d, h * 16 + lax.rem(z + 7, 8) * 2 + c)
    core_peer = (d, m + 1 - 2 * c)

    barrier = pltpu.get_barrier_semaphore()
    everyone = x_peers + y_peers + [hi_peer, z_right, z_left, core_peer]
    for peer in everyone:
        pl.semaphore_signal(barrier, inc=1, device_id=peer, device_id_type=MESH)

    started = []
    slots = []

    def take(n):
        first = len(slots)
        slots.extend([None] * n)
        return first

    def push(src, dst, peer, when=None, at=None):
        n = len(started)
        copy = pltpu.make_async_remote_copy(
            src_ref=src, dst_ref=dst, send_sem=send.at[n],
            recv_sem=recv.at[take(1) if at is None else at],
            device_id=peer, device_id_type=MESH,
        )
        started.append((copy, when))
        if when is None:
            copy.start()
        else:
            pl.when(when)(copy.start)
        return copy

    def arrive(copies):
        for copy in copies:
            copy.wait_recv()

    def expect(dst, at):
        pltpu.make_async_remote_copy(
            src_ref=dst, dst_ref=dst, send_sem=send.at[0], recv_sem=recv.at[at],
            device_id=core_peer, device_id_type=MESH,
        ).wait_recv()

    gain = gain_ref[...][None, :]
    cot_all[z, h, c] = cot_ref[...]
    inputs = up(x_ref[...])
    local_mean = jnp.sum(inputs, 1, keepdims=True) / FEATURES
    local_centre = inputs - local_mean
    local_m2 = jnp.sum(local_centre * local_centre, 1, keepdims=True)
    stats[x, y] = columns_to_rows(local_mean, local_m2)
    bw[:, :384] = wqkv_ref[...]
    bw[:, 384:] = win_ref[...]
    ow[:128] = wo_ref[...]
    ow[128:] = wout_ref[...]
    pl.semaphore_wait(barrier, len(everyone))

    def hi_start(a):
        return [push(a.at[z, h, c], a.at[z, h, c], hi_peer)]

    def ring_start(a, kind, s):
        hh = h if kind == 0 else 1 - h
        right = lax.rem(z + 9 - s, 8)
        left = lax.rem(z + s - 1, 8)
        if s == 4:
            first, second = pl.ds(0, 32), pl.ds(32, 32)
            return [
                push(a.at[right, hh, c, first], a.at[right, hh, c, first], z_right),
                push(a.at[left, hh, c, second], a.at[left, hh, c, second], z_left),
            ]
        return [
            push(a.at[right, hh, c], a.at[right, hh, c], z_right),
            push(a.at[left, hh, c], a.at[left, hh, c], z_left),
        ]

    def core_start(a, s):
        ats = [z] if s == 0 else [lax.rem(z + s, 8)]
        if s in (1, 2, 3):
            ats.append(lax.rem(z + 8 - s, 8))
        return [push(a.at[at, :, c], a.at[at, :, c], core_peer) for at in ats]

    class Gather:
        def __init__(self, a):
            self.a = a
            self.hi = hi_start(a)
            self.own = ring_start(a, 0, 1)
            self.other = None
            self.core = {}

        def first_other(self):
            arrive(self.hi)
            self.other = ring_start(self.a, 1, 1)
            self.core[0] = core_start(self.a, 0)

        def own_step(self, s):
            arrive(self.own)
            self.own = ring_start(self.a, 0, s) if s < 5 else []

        def other_step(self, s):
            arrive(self.other)
            self.other = ring_start(self.a, 1, s) if s < 5 else []
            self.core[s - 1] = core_start(self.a, s - 1)

        def ready(self, s):
            arrive(self.core.pop(s))

    def rows_of(a, yy):
        parts = []
        for xx in range(4):
            at = lax.rem(z + 2 * yy + xx % 2, 8)
            parts.append(a[at, xx // 2].reshape(128, FEATURES))
        return jnp.concatenate(parts, 0)

    class Scatter:
        def __init__(self, part, hl, hr, fl, fr, s, t):
            self.part, self.hl, self.hr, self.fl, self.fr = part, hl, hr, fl, fr
            self.s, self.t = s, t
            self.base = take(4)
            self.half, self.full = {}, {}

        def send_half(self, yy):
            far = around(x, 2)
            first, second = pl.ds(0, 64), pl.ds(64, 64)
            self.half[yy] = [
                push(self.part.at[far, yy, first], self.hl.at[yy], x_right),
                push(self.part.at[far, yy, second], self.hr.at[yy], x_left),
            ]

        def send_full(self, yy):
            arrive(self.half.pop(yy))
            right, left = around(x, 1), around(x, 3)
            new = up(self.part[right, yy, :64]) + up(self.hl[yy])
            self.part[right, yy, :64] = new.astype(BF16)
            a = push(self.part.at[right, yy], self.fl.at[yy], x_right)
            new = up(self.part[left, yy, 64:]) + up(self.hr[yy])
            self.part[left, yy, 64:] = new.astype(BF16)
            b = push(self.part.at[left, yy], self.fr.at[yy], x_left)
            self.full[yy] = [a, b]

        def send_y(self, yy):
            arrive(self.full.pop(yy))
            total = up(self.part[x, yy]) + up(self.fl[yy]) + up(self.fr[yy])
            self.s[yy] = total.astype(BF16)
            o = lax.rem(yy - y + 4, 4)
            slot = lax.rem(o + 3, 4)
            push(
                self.s.at[yy], self.t.at[slot], dp_at(x, yy), when=o != 0, at=self.base + slot
            )

        def result(self):
            total = up(self.part[x, y]) + up(self.fl[y]) + up(self.fr[y])
            for i in range(3):
                expect(self.t.at[i], self.base + i)
                total = total + up(self.t[i])
            return total

    def sums_x(ref):
        return [push(ref.at[x, y], ref.at[x, y], peer) for peer in x_peers]

    def sums_y(ref):
        return [push(ref.at[:, y], ref.at[:, y], peer) for peer in y_peers]

    st = sums_x(stats)
    cg = Gather(cot_all)
    arrive(st)
    st = sums_y(stats)
    cg.first_other()
    cg.own_step(2)
    arrive(st)
    every = stats[...].reshape(16, 8, 128)
    mean_row = jnp.sum(every[:, 0:1, :], 0) / N_DP
    apart = every[:, 0:1, :] - mean_row[None]
    m2_row = jnp.sum(every[:, 1:2, :], 0) + FEATURES * jnp.sum(apart * apart, 0)
    scaling_row = 1.0 / jnp.sqrt(m2_row / D + epsilon)
    mean, scaling = rows_to_columns(mean_row, scaling_row)
    centred = (inputs - mean) * scaling
    nrm_all[z, h, c] = (centred * gain).astype(BF16)
    ng = Gather(nrm_all)
    cen_ref[...] = centred
    scl_ref[...] = jnp.broadcast_to(scaling, (64, 128))

    gs = Scatter(g2, hl2, hr2, fl2, fr2, s2, t2)
    fs = Scatter(fp, hlf, hrf, flf, frf, sf, tf)
    q_base = take(4)

    def g_product(yy):
        product = mm_nt(rows_of(cot_all, yy), ow[...]).astype(BF16)
        g2[:, yy] = product[:, 128:].reshape(4, 128, 384)
        gs.send_half(yy)
        g1[:, yy] = product[:, :128].reshape(4, 128, 128)
        o = lax.rem(yy - y + 4, 4)
        slot = lax.rem(o + 3, 4)
        push(g1.at[:, yy], rg1.at[slot], dp_at(x, yy), when=o != 0, at=q_base + slot)

    def f_product(yy):
        product = mm(rows_of(nrm_all, yy), bw[...]).astype(BF16)
        fp[:, yy] = product.reshape(4, 128, 768)
        fs.send_half(yy)

    cg.other_step(2)
    cg.own_step(3)
    ng.first_other()
    ng.own_step(2)
    cg.other_step(3)
    cg.own_step(4)
    cg.ready(0)
    cg.ready(1)
    g_product(0)
    ng.other_step(2)
    ng.own_step(3)
    cg.other_step(4)
    cg.own_step(5)
    cg.ready(2)
    g_product(3)
    gs.send_full(0)
    ng.other_step(3)
    ng.own_step(4)
    cg.other_step(5)
    cg.ready(3)
    g_product(1)
    gs.send_full(3)
    ng.ready(0)
    ng.ready(1)
    f_product(0)
    gs.send_y(0)
    ng.other_step(4)
    ng.own_step(5)
    cg.ready(4)
    g_product(2)
    gs.send_full(1)
    ng.ready(2)
    f_product(3)
    fs.send_full(0)
    gs.send_y(3)
    ng.other_step(5)
    gs.send_full(2)
    ng.ready(3)
    f_product(1)
    fs.send_full(3)
    gs.send_y(1)
    fs.send_y(0)
    ng.ready(4)
    f_product(2)
    fs.send_full(1)
    gs.send_y(2)
    fs.send_y(3)
    fs.send_full(2)
    total = up(g1[:, y])
    for i in range(3):
        expect(rg1.at[i], q_base + i)
        total = total + up(rg1[i])
    s1[...] = total.astype(BF16)
    tq = [push(s1.at[around(x, o)], tg1.at[o - 1], x_peers[o - 1]) for o in (1, 2, 3)]
    fs.send_y(1)
    grad_act = gs.result()
    arrive(tq)
    grad_attn = up(g1[x, y]) + up(tg1[0]) + up(tg1[1]) + up(tg1[2])
    for i in range(3):
        grad_attn = grad_attn + up(rg1[i, x])
    fs.send_y(2)
    features = fs.result()

    qg, kg = qg_ref[...], kg_ref[...]
    queries, query_unit, query_scale = head_norm(features[:, :128], qg)
    keys, key_unit, key_scale = head_norm(features[:, 128:256], kg)
    query_b, key_b = queries.astype(BF16), keys.astype(BF16)
    value_b = features[:, 256:384].astype(BF16)
    pre = features[:, 384:]
    expo = jnp.exp(mm_nt(query_b, key_b) * FACTOR)
    prob = expo / jnp.sum(expo, -1, keepdims=True)
    prob_b = prob.astype(BF16)
    inner = GELU_ROOT * (pre + GELU_CUBE * (pre * pre * pre))
    bend = jnp.tanh(inner)
    m_all[x, y, :, :128] = mm(prob_b, value_b).astype(BF16)
    m_all[x, y, :, 128:] = (0.5 * pre * (1.0 + bend)).astype(BF16)
    own_m = m_all.at[x, y]
    m_y = [push(own_m, own_m, peer) for peer in y_peers]

    class Spread:
        def __init__(self, a):
            self.a, self.near, self.far = a, {}, {}

        def send_near(self, k, yy):
            block = self.a.at[x, yy]
            self.near[k] = [push(block, block, x_right), push(block, block, x_left)]

        def send_far(self, k, yy):
            arrive(self.near.pop(k))
            first = self.a.at[around(x, 3), yy, pl.ds(0, 64)]
            second = self.a.at[around(x, 1), yy, pl.ds(64, 64)]
            self.far[k] = [push(first, first, x_right), push(second, second, x_left)]

        def ready(self, k):
            arrive(self.far.pop(k))

    ms = Spread(m_all)
    ms.send_near(0, y)
    slope = 0.5 * (1.0 + bend) + 0.5 * pre * (1.0 - bend * bend) * (
        GELU_ROOT * (1.0 + 3.0 * GELU_CUBE * (pre * pre))
    )
    grad_attn = grad_attn.astype(BF16)
    rb_all[x, y, :, 256:] = (grad_act * slope).astype(BF16)
    dprob = mm_nt(grad_attn, value_b)
    delta = jnp.sum(prob * dprob, -1, keepdims=True)
    dscore = (prob * (dprob - delta)).astype(BF16)
    grad_qn = mm(dscore, key_b) * FACTOR
    grad_kn = mm_tn(dscore, query_b) * FACTOR
    ra_all[x, y] = head_back(grad_qn, query_unit, query_scale, qg).astype(BF16)
    rb_all[x, y, :, :128] = head_back(grad_kn, key_unit, key_scale, kg).astype(BF16)
    rb_all[x, y, :, 128:256] = mm_tn(prob_b, grad_attn).astype(BF16)
    own_a, own_b = ra_all.at[x, y], rb_all.at[x, y]
    a_x = [push(own_a, own_a, peer) for peer in x_peers]
    b_base = take(4)
    for o in (1, 2, 3):
        push(own_b, own_b, y_peers[o - 1], at=b_base + o - 1)
    rs = Spread(rb_all)

    def r_near(yy):
        o = lax.rem(y - yy + 4, 4)

        @pl.when(o != 0)
        def _():
            expect(rb_all.at[x, yy], b_base + lax.rem(o + 3, 4))

        rs.send_near(yy, yy)

    for o in (1, 2, 3):
        arrive([m_y[o - 1]])
        ms.send_near(o, around(y, 4 - o))
        ms.send_far(o - 1, around(y, 5 - o))
    arrive(a_x)
    a_y = [push(ra_all.at[:, y], ra_all.at[:, y], peer) for peer in y_peers]
    r_near(2)
    ms.send_far(3, around(y, 1))
    r_near(1)
    for k in range(4):
        ms.ready(k)

    class Reduce:
        def __init__(self, e, r, s, left, right, f, yv, got):
            self.e, self.r, self.s, self.left, self.right = e, r, s, left, right
            self.f, self.yv, self.got = f, yv, got
            self.core, self.ring = {}, None

        def chunk(self, yy, part):
            self.e[yy] = part.astype(BF16).reshape(4, 2, 64, FEATURES)
            self.core[yy] = [push(self.e.at[yy, :, 1 - c], self.r.at[yy], core_peer)]

        def core_sum(self, yy):
            arrive(self.core.pop(yy))
            own = self.e[yy, :, pl.ds(c, 1)].reshape(4, 64, FEATURES)
            total = (up(own) + up(self.r[yy])).astype(BF16)
            for xx in range(4):
                self.s[2 * yy + xx % 2, xx // 2] = total[xx]

        def step(self, s):
            if s == 1:
                first, second = pl.ds(0, 32), pl.ds(32, 32)
                self.ring = [
                    push(self.s.at[4, :, first], self.left.at[0, :, first], z_right),
                    push(self.s.at[4, :, second], self.right.at[0, :, second], z_left),
                ]
                return
            first, second = (slice(0, 32), slice(32, 64)) if s == 2 else (slice(None),) * 2
            a, b = self.ring
            arrive([a])
            new = up(self.s[5 - s, :, first]) + up(self.left[s - 2, :, first])
            self.s[5 - s, :, first] = new.astype(BF16)
            a = push(self.s.at[5 - s], self.left.at[s - 1], z_right)
            arrive([b])
            new = up(self.s[3 + s, :, second]) + up(self.right[s - 2, :, second])
            self.s[3 + s, :, second] = new.astype(BF16)
            b = push(self.s.at[3 + s], self.right.at[s - 1], z_left)
            self.ring = [a, b]

        def last(self):
            arrive(self.ring)
            self.f[...] = up(self.s[0]) + up(self.left[3]) + up(self.right[3])
            self.yv[...] = self.f[1 - h].astype(BF16)
            self.hi = [push(self.yv, self.got, hi_peer)]

        def result(self):
            arrive(self.hi)
            return self.f[h] + up(self.got[...])

    outs = Reduce(eo, reo, so, lo, ro, fo, yo, ryo)
    grads = Reduce(eg, reg, sg, lg, rg, fg, yg, ryg)

    def grad_product(yy):
        rs.ready(yy)
        part = mm_nt(ra_all[:, yy].reshape(512, 128), bw[:, :128])
        part = part + mm_nt(rb_all[:, yy].reshape(512, 640), bw[:, 128:])
        grads.chunk(yy, part)

    for yy in SCATTER_ORDER:
        outs.chunk(yy, mm(m_all[:, yy].reshape(512, 512), ow[...]))
    rs.send_far(2, 2)
    r_near(3)
    for yy in SCATTER_ORDER:
        outs.core_sum(yy)
    outs.step(1)
    rs.send_far(1, 1)
    r_near(0)
    weight = jnp.zeros((512, FEATURES), F32)
    for yy in range(4):
        weight = weight + mm_tn(m_all[:, yy].reshape(512, 512), rows_of(cot_all, yy))
    gwo_ref[...] = weight[:128].astype(BF16)
    gwout_ref[...] = weight[128:].astype(BF16)
    outs.step(2)
    arrive(a_y)
    grad_product(2)
    rs.send_far(3, 3)
    outs.step(3)
    grad_product(1)
    grads.core_sum(2)
    grads.step(1)
    rs.send_far(0, 0)
    outs.step(4)
    grad_product(3)
    grads.core_sum(1)
    grads.step(2)
    outs.last()
    grad_product(0)
    grads.core_sum(3)
    grads.step(3)
    normed_rows = [rows_of(nrm_all, yy) for yy in range(4)]
    weight = jnp.zeros((FEATURES, 128), F32)
    for yy in range(4):
        weight = weight + mm_tn(normed_rows[yy], ra_all[:, yy].reshape(512, 128))
    gwqkv_ref[:, :128] = weight.astype(BF16)
    out_ref[...] = (up(x_ref[...]) + outs.result()).astype(BF16)
    grads.core_sum(0)
    grads.step(4)
    weight = jnp.zeros((FEATURES, 640), F32)
    for yy in range(4):
        weight = weight + mm_tn(normed_rows[yy], rb_all[:, yy].reshape(512, 640))
    gwqkv_ref[:, 128:] = weight[:, :256].astype(BF16)
    gwin_ref[...] = weight[:, 256:].astype(BF16)
    grads.last()
    local_grad = grads.result() * gain
    centred = cen_ref[...]
    stats_b[x, y] = columns_to_rows(
        jnp.sum(local_grad, 1, keepdims=True),
        jnp.sum(local_grad * centred, 1, keepdims=True),
    )
    arrive(sums_x(stats_b))
    arrive(sums_y(stats_b))
    sums = jnp.sum(stats_b[...].reshape(16, 8, 128), 0) / D
    first, second = rows_to_columns(sums[0:1], sums[1:2])
    scaling = scl_ref[...][:, 0:1]
    gx_ref[...] = (
        up(cot_ref[...]) + scaling * (local_grad - first - centred * second)
    ).astype(BF16)
    for copy, when in started:
        if when is None:
            copy.wait_send()
        else:
            pl.when(when)(copy.wait_send)


def place(*refs):
    n = len(refs) // 2
    for i in range(n):
        refs[n + i][...] = refs[i][...]


def shards(block_input, ln_gain, w_qkv, w_in, w_o, w_out, q_gain, k_gain, cotangent):
    def vmem(*shape):
        return pltpu.VMEM(shape, BF16)

    def scatter(cols):
        return [
            vmem(4, 4, 128, cols), vmem(4, 64, cols), vmem(4, 64, cols),
            vmem(4, 128, cols), vmem(4, 128, cols), vmem(4, 128, cols), vmem(4, 128, cols),
        ]

    ring = vmem(4, 2, 64, 384)
    scratch = [
        vmem(8, 2, 2, 64, 384), vmem(8, 2, 2, 64, 384), vmem(384, 768), vmem(512, 384),
        pltpu.VMEM((4, 4, 8, 128), F32), pltpu.VMEM((4, 4, 8, 128), F32),
        pltpu.VMEM((64, 384), F32), pltpu.VMEM((64, 128), F32),
        vmem(4, 4, 128, 128), vmem(4, 4, 128, 128), vmem(4, 128, 128), vmem(3, 128, 128),
        *scatter(384), *scatter(768),
        vmem(4, 4, 128, 512), vmem(4, 4, 128, 128), vmem(4, 4, 128, 640),
        vmem(4, 4, 2, 64, 384), vmem(4, 4, 2, 64, 384), vmem(4, 4, 64, 384), vmem(4, 4, 64, 384),
        vmem(8, 2, 64, 384), vmem(8, 2, 64, 384), ring, ring, ring, ring,
        pltpu.VMEM((2, 64, 384), F32), pltpu.VMEM((2, 64, 384), F32),
        vmem(64, 384), vmem(64, 384), vmem(64, 384), vmem(64, 384),
        pltpu.SemaphoreType.DMA((COPIES,)), pltpu.SemaphoreType.DMA((COPIES,)),
    ]
    args = (block_input, cotangent, ln_gain, w_qkv, w_in, w_o, w_out, q_gain, k_gain)
    outs = (block_input, cotangent, w_qkv, w_in, w_o, w_out)
    shapes = tuple(jax.ShapeDtypeStruct(a.shape, BF16) for a in outs)
    results = pl.pallas_call(
        kernel,
        out_shape=shapes,
        in_specs=[pl.BlockSpec(memory_space=pltpu.VMEM)] * len(args),
        out_specs=tuple(pl.BlockSpec(memory_space=pltpu.VMEM) for _ in outs),
        scratch_shapes=scratch,
        compiler_params=pltpu.CompilerParams(
            collective_id=1, has_side_effects=True, vmem_limit_bytes=56 * 2**20
        ),
        name="block",
    )(*args)
    return pl.pallas_call(
        place,
        out_shape=shapes,
        in_specs=[pl.BlockSpec(memory_space=pltpu.VMEM)] * len(outs),
        out_specs=tuple(pl.BlockSpec(memory_space=pltpu.VMEM) for _ in outs),
        name="place",
    )(*results)


def solution(mesh):
    return jax.shard_map(
        shards,
        mesh=mesh,
        in_specs=(
            P("mp", "dp"),
            P("dp"),
            P("dp", "mp"),
            P("dp", "mp"),
            P("mp", "dp"),
            P("mp", "dp"),
            P("mp", None),
            P("mp", None),
            P("mp", "dp"),
        ),
        out_specs=(
            P("mp", "dp"),
            P("mp", "dp"),
            P("dp", "mp"),
            P("dp", "mp"),
            P("mp", "dp"),
            P("mp", "dp"),
        ),
        check_vma=False,
    )
```

time: 196 us -> 172 us (0.88)
  Pallas kernels: 188 us -> 171 us
  local copies, waits for them, and re-layouts: 7.38 us -> 0 us
    pallas_call x1 -> x2, Pallas kernels: 188 us -> 171 us  [the longest x1 169 us: shards(): pl.pallas_call(kernel, out_shape=shapes, in_specs=[pl.BlockSpec(memory_sp...]
    unnamed x14 -> x0, local copies, waits for them, and re-layouts: 6.13 us -> none
where the time goes in v2:
time: 172 us
  Pallas kernels  171 us (99%)
    pallas_call x1, Pallas kernels, shards(): pl.pallas_call(kernel, out_shape=shapes, in_specs=[pl.BlockSpec(memory_sp...  169 us

profile of v2, /device:TPU:6, one launch (start us, length us, event | category | flops | bytes accessed | tf_op | source)
XLA Modules:
  0.0 171.7 jit_solution(14882483891772703790)
XLA Ops:
  0.6 168.9 %block.1 = (bf16[64,384]{1,0:T(8,128)(2,1)}, bf16[64,384]{1,0:T(8,128)(2,1)}, bf16[384,384]{1,0:T(8,128)(2,1)}, bf16[384,384]{1,0:T(8,128)(2,1)}, bf16[128,384]{1,0:T(8,128)(2,1)}, /*index=5*/bf16[384,384]{1,0:T(8,128)(2,1)}) custom-call(bf16[64,384]{1,0:T(8,128)(2,1)} %x_ref.1, bf16[64,384]{1,0:T(8,128)(2,1)} %cot_ref.1, f32[384]{0:T(512)} %gain_ref.1, ...), custom_call_target="tpu_custom_call" | custom-call | tf_op jit(solution)/shard_map/block/pallas_call | solution.py:587
  169.5 2.2 %place.1 = (bf16[64,384]{1,0:T(8,128)(2,1)}, bf16[64,384]{1,0:T(8,128)(2,1)}, bf16[384,384]{1,0:T(8,128)(2,1)}, bf16[384,384]{1,0:T(8,128)(2,1)}, bf16[128,384]{1,0:T(8,128)(2,1)}, /*index=5*/bf16[384,384]{1,0:T(8,128)(2,1)}) custom-call(bf16[64,384]{1,0:T(8,128)(2,1)} %get-tuple-element.12.refs_0_, bf16[64,384]{1,0:T(8,128)(2,1)} %get-tuple-element.13.refs_1_, ...), custom_call_target="tpu_custom_call" | custom-call | tf_op jit(solution)/shard_map/place/pallas_call | solution.py:598

commit v3 on v2

--- a/solution.py
+++ b/solution.py
@@ -19,8 +19,8 @@
 GELU_CUBE = 0.044715
 NT = (((1,), (1,)), ((), ()))
 TN = (((0,), (0,)), ((), ()))
-COPIES = 300
-GATHER_ORDER = (0, 3, 1, 2)
+SENDS = 64
+ARRIVALS = 188
 SCATTER_ORDER = (2, 1, 3, 0)
 
 
@@ -73,10 +73,10 @@
     x_ref, cot_ref, gain_ref, wqkv_ref, win_ref, wo_ref, wout_ref, qg_ref, kg_ref,
     out_ref, gx_ref, gwqkv_ref, gwin_ref, gwo_ref, gwout_ref,
     cot_all, nrm_all, bw, ow, stats, stats_b, cen_ref, scl_ref,
-    g1, rg1, s1, tg1,
     g2, hl2, hr2, fl2, fr2, s2, t2,
     fp, hlf, hrf, flf, frf, sf, tf,
-    m_all, ra_all, rb_all, eo, eg, reo, reg, so, sg, lo, ro, lg, rg, fo, fg, yo, yg, ryo, ryg,
+    ep, hle, hre, fle, fre, se, te,
+    m_all, r_all, eo, eg, reo, reg, so, sg, lo, ro, lg, rg, fo, fg, yo, yg, ryo, ryg,
     send, recv,
 ):
     d = lax.axis_index("dp")
@@ -111,10 +111,18 @@
         slots.extend([None] * n)
         return first
 
+    def finish(copy, when):
+        if when is None:
+            copy.wait_send()
+        else:
+            pl.when(when)(copy.wait_send)
+
     def push(src, dst, peer, when=None, at=None):
         n = len(started)
+        if n >= SENDS:
+            finish(*started[n - SENDS])
         copy = pltpu.make_async_remote_copy(
-            src_ref=src, dst_ref=dst, send_sem=send.at[n],
+            src_ref=src, dst_ref=dst, send_sem=send.at[n % SENDS],
             recv_sem=recv.at[take(1) if at is None else at],
             device_id=peer, device_id_type=MESH,
         )
@@ -274,21 +282,19 @@
 
     gs = Scatter(g2, hl2, hr2, fl2, fr2, s2, t2)
     fs = Scatter(fp, hlf, hrf, flf, frf, sf, tf)
-    q_base = take(4)
+    es = Scatter(ep, hle, hre, fle, fre, se, te)
 
     def g_product(yy):
         product = mm_nt(rows_of(cot_all, yy), ow[...]).astype(BF16)
-        g2[:, yy] = product[:, 128:].reshape(4, 128, 384)
+        g2[:, yy] = product.reshape(4, 128, 512)
         gs.send_half(yy)
-        g1[:, yy] = product[:, :128].reshape(4, 128, 128)
-        o = lax.rem(yy - y + 4, 4)
-        slot = lax.rem(o + 3, 4)
-        push(g1.at[:, yy], rg1.at[slot], dp_at(x, yy), when=o != 0, at=q_base + slot)
 
     def f_product(yy):
         product = mm(rows_of(nrm_all, yy), bw[...]).astype(BF16)
-        fp[:, yy] = product.reshape(4, 128, 768)
+        fp[:, yy] = product[:, :384].reshape(4, 128, 384)
         fs.send_half(yy)
+        ep[:, yy] = product[:, 384:].reshape(4, 128, 384)
+        es.send_half(yy)
 
     cg.other_step(2)
     cg.own_step(3)
@@ -309,125 +315,148 @@
     ng.other_step(3)
     ng.own_step(4)
     cg.other_step(5)
-    cg.ready(3)
-    g_product(1)
-    gs.send_full(3)
     ng.ready(0)
     ng.ready(1)
     f_product(0)
+    gs.send_full(3)
     gs.send_y(0)
     ng.other_step(4)
     ng.own_step(5)
-    cg.ready(4)
-    g_product(2)
-    gs.send_full(1)
     ng.ready(2)
     f_product(3)
     fs.send_full(0)
+    es.send_full(0)
+    ng.other_step(5)
     gs.send_y(3)
-    ng.other_step(5)
-    gs.send_full(2)
     ng.ready(3)
     f_product(1)
     fs.send_full(3)
-    gs.send_y(1)
+    es.send_full(3)
     fs.send_y(0)
     ng.ready(4)
     f_product(2)
+    es.send_y(0)
     fs.send_full(1)
-    gs.send_y(2)
+    es.send_full(1)
     fs.send_y(3)
+    cg.ready(3)
+    cg.ready(4)
+    g_product(1)
     fs.send_full(2)
-    total = up(g1[:, y])
-    for i in range(3):
-        expect(rg1.at[i], q_base + i)
-        total = total + up(rg1[i])
-    s1[...] = total.astype(BF16)
-    tq = [push(s1.at[around(x, o)], tg1.at[o - 1], x_peers[o - 1]) for o in (1, 2, 3)]
+    es.send_full(2)
+    es.send_y(3)
+    g_product(2)
     fs.send_y(1)
-    grad_act = gs.result()
-    arrive(tq)
-    grad_attn = up(g1[x, y]) + up(tg1[0]) + up(tg1[1]) + up(tg1[2])
-    for i in range(3):
-        grad_attn = grad_attn + up(rg1[i, x])
+    es.send_y(1)
+    gs.send_full(1)
     fs.send_y(2)
-    features = fs.result()
+    es.send_y(2)
+    gs.send_full(2)
+    gs.send_y(1)
+    qkv = fs.result()
 
     qg, kg = qg_ref[...], kg_ref[...]
-    queries, query_unit, query_scale = head_norm(features[:, :128], qg)
-    keys, key_unit, key_scale = head_norm(features[:, 128:256], kg)
+    queries, query_unit, query_scale = head_norm(qkv[:, :128], qg)
+    keys, key_unit, key_scale = head_norm(qkv[:, 128:256], kg)
     query_b, key_b = queries.astype(BF16), keys.astype(BF16)
-    value_b = features[:, 256:384].astype(BF16)
-    pre = features[:, 384:]
+    value_b = qkv[:, 256:].astype(BF16)
     expo = jnp.exp(mm_nt(query_b, key_b) * FACTOR)
     prob = expo / jnp.sum(expo, -1, keepdims=True)
     prob_b = prob.astype(BF16)
+    m_all[x, y, :, :128] = mm(prob_b, value_b).astype(BF16)
+    pre = es.result()
     inner = GELU_ROOT * (pre + GELU_CUBE * (pre * pre * pre))
     bend = jnp.tanh(inner)
-    m_all[x, y, :, :128] = mm(prob_b, value_b).astype(BF16)
     m_all[x, y, :, 128:] = (0.5 * pre * (1.0 + bend)).astype(BF16)
-    own_m = m_all.at[x, y]
-    m_y = [push(own_m, own_m, peer) for peer in y_peers]
 
     class Spread:
         def __init__(self, a):
-            self.a, self.near, self.far = a, {}, {}
-
-        def send_near(self, k, yy):
+            self.a = a
+            self.line, self.near, self.far = take(4), take(8), take(8)
+            own = a.at[x, y]
+            push(own, own, dp_at(x, lax.min(y + 1, 3)), when=y < 3, at=self.line + y)
+            push(own, own, dp_at(x, lax.max(y - 1, 0)), when=y > 0, at=self.line + y)
+
+        def along_y(self, s, then=None):
+            for sign in (-1, 1):
+                there = y + sign * s
+                yy = lax.rem(there + 4, 4)
+                here = (there >= 0) & (there < 4)
+                block = self.a.at[x, yy]
+
+                @pl.when(here)
+                def _():
+                    expect(block, self.line + yy)
+
+                on = y - sign
+                push(
+                    block, block, dp_at(x, lax.clamp(0, on, 3)),
+                    when=here & (on >= 0) & (on < 4), at=self.line + yy,
+                )
+                if then is not None:
+                    then(yy, here)
+
+        def send_near(self, yy, when=None):
             block = self.a.at[x, yy]
-            self.near[k] = [push(block, block, x_right), push(block, block, x_left)]
-
-        def send_far(self, k, yy):
-            arrive(self.near.pop(k))
-            first = self.a.at[around(x, 3), yy, pl.ds(0, 64)]
-            second = self.a.at[around(x, 1), yy, pl.ds(64, 64)]
-            self.far[k] = [push(first, first, x_right), push(second, second, x_left)]
-
-        def ready(self, k):
-            arrive(self.far.pop(k))
+            push(block, block, x_right, when=when, at=self.near + yy)
+            push(block, block, x_left, when=when, at=self.near + 4 + yy)
+
+        def send_far(self, yy, when=None):
+            first = self.a.at[around(x, 3), yy]
+            second = self.a.at[around(x, 1), yy]
+
+            def wait():
+                expect(first, self.near + yy)
+                expect(second, self.near + 4 + yy)
+
+            if when is None:
+                wait()
+            else:
+                pl.when(when)(wait)
+            first, second = first.at[pl.ds(0, 64)], second.at[pl.ds(64, 64)]
+            push(first, first, x_right, when=when, at=self.far + yy)
+            push(second, second, x_left, when=when, at=self.far + 4 + yy)
+
+        def far_step(self, s):
+            for sign in (-1, 1):
+                there = y + sign * s
+                self.send_far(lax.rem(there + 4, 4), (there >= 0) & (there < 4))
+
+        def ready(self, yy):
+            far = self.a.at[around(x, 2), yy]
+            expect(far.at[pl.ds(0, 64)], self.far + yy)
+            expect(far.at[pl.ds(64, 64)], self.far + 4 + yy)
 
     ms = Spread(m_all)
-    ms.send_near(0, y)
+    ms.send_near(y)
     slope = 0.5 * (1.0 + bend) + 0.5 * pre * (1.0 - bend * bend) * (
         GELU_ROOT * (1.0 + 3.0 * GELU_CUBE * (pre * pre))
     )
-    grad_attn = grad_attn.astype(BF16)
-    rb_all[x, y, :, 256:] = (grad_act * slope).astype(BF16)
+    gs.send_y(2)
+    grad_mixed = gs.result()
+    grad_attn = grad_mixed[:, :128].astype(BF16)
+    r_all[x, y, :, 384:] = (grad_mixed[:, 128:] * slope).astype(BF16)
     dprob = mm_nt(grad_attn, value_b)
     delta = jnp.sum(prob * dprob, -1, keepdims=True)
     dscore = (prob * (dprob - delta)).astype(BF16)
     grad_qn = mm(dscore, key_b) * FACTOR
     grad_kn = mm_tn(dscore, query_b) * FACTOR
-    ra_all[x, y] = head_back(grad_qn, query_unit, query_scale, qg).astype(BF16)
-    rb_all[x, y, :, :128] = head_back(grad_kn, key_unit, key_scale, kg).astype(BF16)
-    rb_all[x, y, :, 128:256] = mm_tn(prob_b, grad_attn).astype(BF16)
-    own_a, own_b = ra_all.at[x, y], rb_all.at[x, y]
-    a_x = [push(own_a, own_a, peer) for peer in x_peers]
-    b_base = take(4)
-    for o in (1, 2, 3):
-        push(own_b, own_b, y_peers[o - 1], at=b_base + o - 1)
-    rs = Spread(rb_all)
-
-    def r_near(yy):
-        o = lax.rem(y - yy + 4, 4)
-
-        @pl.when(o != 0)
-        def _():
-            expect(rb_all.at[x, yy], b_base + lax.rem(o + 3, 4))
-
-        rs.send_near(yy, yy)
-
-    for o in (1, 2, 3):
-        arrive([m_y[o - 1]])
-        ms.send_near(o, around(y, 4 - o))
-        ms.send_far(o - 1, around(y, 5 - o))
-    arrive(a_x)
-    a_y = [push(ra_all.at[:, y], ra_all.at[:, y], peer) for peer in y_peers]
-    r_near(2)
-    ms.send_far(3, around(y, 1))
-    r_near(1)
-    for k in range(4):
-        ms.ready(k)
+    r_all[x, y, :, :128] = head_back(grad_qn, query_unit, query_scale, qg).astype(BF16)
+    r_all[x, y, :, 128:256] = head_back(grad_kn, key_unit, key_scale, kg).astype(BF16)
+    r_all[x, y, :, 256:384] = mm_tn(prob_b, grad_attn).astype(BF16)
+    rs = Spread(r_all)
+    rs.send_near(y)
+    ms.along_y(1, ms.send_near)
+    ms.send_far(y)
+    rs.along_y(1)
+    ms.along_y(2, ms.send_near)
+    ms.far_step(1)
+    rs.along_y(2)
+    ms.along_y(3, ms.send_near)
+    ms.far_step(2)
+    rs.send_near(2, y != 2)
+    ms.far_step(3)
+    rs.send_near(1, y != 1)
 
     class Reduce:
         def __init__(self, e, r, s, left, right, f, yv, got):
@@ -481,55 +510,56 @@
 
     def grad_product(yy):
         rs.ready(yy)
-        part = mm_nt(ra_all[:, yy].reshape(512, 128), bw[:, :128])
-        part = part + mm_nt(rb_all[:, yy].reshape(512, 640), bw[:, 128:])
-        grads.chunk(yy, part)
-
-    for yy in SCATTER_ORDER:
+        grads.chunk(yy, mm_nt(r_all[:, yy].reshape(512, 768), bw[...]))
+
+    def out_product(yy):
+        ms.ready(yy)
         outs.chunk(yy, mm(m_all[:, yy].reshape(512, 512), ow[...]))
-    rs.send_far(2, 2)
-    r_near(3)
-    for yy in SCATTER_ORDER:
-        outs.core_sum(yy)
+
+    out_product(2)
+    rs.along_y(3)
+    rs.send_near(3, y != 3)
+    out_product(1)
+    rs.send_far(2)
+    outs.core_sum(2)
     outs.step(1)
-    rs.send_far(1, 1)
-    r_near(0)
+    out_product(3)
+    rs.send_near(0, y != 0)
+    out_product(0)
+    rs.send_far(1)
+    outs.core_sum(1)
+    outs.core_sum(3)
+    outs.core_sum(0)
+    outs.step(2)
+    rs.send_far(3)
+    grad_product(2)
+    rs.send_far(0)
+    grads.core_sum(2)
+    grads.step(1)
+    outs.step(3)
+    grad_product(1)
+    grads.core_sum(1)
+    grads.step(2)
+    outs.step(4)
+    grad_product(3)
+    grads.core_sum(3)
+    grads.step(3)
+    grad_product(0)
+    grads.core_sum(0)
+    grads.step(4)
+    outs.last()
+    weight = jnp.zeros((FEATURES, 768), F32)
+    for yy in range(4):
+        weight = weight + mm_tn(rows_of(nrm_all, yy), r_all[:, yy].reshape(512, 768))
+    gwqkv_ref[...] = weight[:, :384].astype(BF16)
+    gwin_ref[...] = weight[:, 384:].astype(BF16)
+    grads.last()
     weight = jnp.zeros((512, FEATURES), F32)
     for yy in range(4):
         weight = weight + mm_tn(m_all[:, yy].reshape(512, 512), rows_of(cot_all, yy))
     gwo_ref[...] = weight[:128].astype(BF16)
     gwout_ref[...] = weight[128:].astype(BF16)
-    outs.step(2)
-    arrive(a_y)
-    grad_product(2)
-    rs.send_far(3, 3)
-    outs.step(3)
-    grad_product(1)
-    grads.core_sum(2)
-    grads.step(1)
-    rs.send_far(0, 0)
-    outs.step(4)
-    grad_product(3)
-    grads.core_sum(1)
-    grads.step(2)
-    outs.last()
-    grad_product(0)
-    grads.core_sum(3)
-    grads.step(3)
-    normed_rows = [rows_of(nrm_all, yy) for yy in range(4)]
-    weight = jnp.zeros((FEATURES, 128), F32)
-    for yy in range(4):
-        weight = weight + mm_tn(normed_rows[yy], ra_all[:, yy].reshape(512, 128))
-    gwqkv_ref[:, :128] = weight.astype(BF16)
     out_ref[...] = (up(x_ref[...]) + outs.result()).astype(BF16)
-    grads.core_sum(0)
-    grads.step(4)
-    weight = jnp.zeros((FEATURES, 640), F32)
-    for yy in range(4):
-        weight = weight + mm_tn(normed_rows[yy], rb_all[:, yy].reshape(512, 640))
-    gwqkv_ref[:, 128:] = weight[:, :256].astype(BF16)
-    gwin_ref[...] = weight[:, 256:].astype(BF16)
-    grads.last()
     local_grad = grads.result() * gain
     centred = cen_ref[...]
     stats_b[x, y] = columns_to_rows(
@@ -544,11 +574,8 @@
     gx_ref[...] = (
         up(cot_ref[...]) + scaling * (local_grad - first - centred * second)
     ).astype(BF16)
-    for copy, when in started:
-        if when is None:
-            copy.wait_send()
-        else:
-            pl.when(when)(copy.wait_send)
+    for copy, when in started[-SENDS:]:
+        finish(copy, when)
 
 
 def place(*refs):
@@ -572,14 +599,13 @@
         vmem(8, 2, 2, 64, 384), vmem(8, 2, 2, 64, 384), vmem(384, 768), vmem(512, 384),
         pltpu.VMEM((4, 4, 8, 128), F32), pltpu.VMEM((4, 4, 8, 128), F32),
         pltpu.VMEM((64, 384), F32), pltpu.VMEM((64, 128), F32),
-        vmem(4, 4, 128, 128), vmem(4, 4, 128, 128), vmem(4, 128, 128), vmem(3, 128, 128),
-        *scatter(384), *scatter(768),
-        vmem(4, 4, 128, 512), vmem(4, 4, 128, 128), vmem(4, 4, 128, 640),
+        *scatter(512), *scatter(384), *scatter(384),
+        vmem(4, 4, 128, 512), vmem(4, 4, 128, 768),
         vmem(4, 4, 2, 64, 384), vmem(4, 4, 2, 64, 384), vmem(4, 4, 64, 384), vmem(4, 4, 64, 384),
         vmem(8, 2, 64, 384), vmem(8, 2, 64, 384), ring, ring, ring, ring,
         pltpu.VMEM((2, 64, 384), F32), pltpu.VMEM((2, 64, 384), F32),
         vmem(64, 384), vmem(64, 384), vmem(64, 384), vmem(64, 384),
-        pltpu.SemaphoreType.DMA((COPIES,)), pltpu.SemaphoreType.DMA((COPIES,)),
+        pltpu.SemaphoreType.DMA((SENDS,)), pltpu.SemaphoreType.DMA((ARRIVALS,)),
     ]
     args = (block_input, cotangent, ln_gain, w_qkv, w_in, w_o, w_out, q_gain, k_gain)
     outs = (block_input, cotangent, w_qkv, w_in, w_o, w_out)

time: 172 us -> 158 us (0.919)
  Pallas kernels: 171 us -> 156 us
    pallas_call x1, Pallas kernels: 169 us -> 154 us  [shards(): pl.pallas_call(kernel, out_shape=shapes, in_specs=[pl.BlockSpec(memory_sp...]
where the time goes in v3:
time: 158 us; the launch traced here: 157 us
  Pallas kernels  156 us (99%)
    pallas_call x1, Pallas kernels, shards(): pl.pallas_call(kernel, out_shape=shapes, in_specs=[pl.BlockSpec(memory_sp...  154 us

profile of v3, /device:TPU:6, one launch (start us, length us, event | category | flops | bytes accessed | tf_op | source)
XLA Modules:
  0.0 156.8 jit_solution(15830219871280654913)
XLA Ops:
  0.6 153.9 %block.1 = (bf16[64,384]{1,0:T(8,128)(2,1)}, bf16[64,384]{1,0:T(8,128)(2,1)}, bf16[384,384]{1,0:T(8,128)(2,1)}, bf16[384,384]{1,0:T(8,128)(2,1)}, bf16[128,384]{1,0:T(8,128)(2,1)}, /*index=5*/bf16[384,384]{1,0:T(8,128)(2,1)}) custom-call(bf16[64,384]{1,0:T(8,128)(2,1)} %x_ref.1, bf16[64,384]{1,0:T(8,128)(2,1)} %cot_ref.1, f32[384]{0:T(512)} %gain_ref.1, ...), custom_call_target="tpu_custom_call" | custom-call | tf_op jit(solution)/shard_map/block/pallas_call | solution.py:613
  154.6 2.2 %place.1 = (bf16[64,384]{1,0:T(8,128)(2,1)}, bf16[64,384]{1,0:T(8,128)(2,1)}, bf16[384,384]{1,0:T(8,128)(2,1)}, bf16[384,384]{1,0:T(8,128)(2,1)}, bf16[128,384]{1,0:T(8,128)(2,1)}, /*index=5*/bf16[384,384]{1,0:T(8,128)(2,1)}) custom-call(bf16[64,384]{1,0:T(8,128)(2,1)} %get-tuple-element.12.refs_0_, bf16[64,384]{1,0:T(8,128)(2,1)} %get-tuple-element.13.refs_1_, ...), custom_call_target="tpu_custom_call" | custom-call | tf_op jit(solution)/shard_map/place/pallas_call | solution.py:624

commit v4 on v3

--- a/solution.py
+++ b/solution.py
@@ -19,8 +19,8 @@
 GELU_CUBE = 0.044715
 NT = (((1,), (1,)), ((), ()))
 TN = (((0,), (0,)), ((), ()))
-SENDS = 64
-ARRIVALS = 188
+SENDS = 32
+ARRIVALS = 208
 SCATTER_ORDER = (2, 1, 3, 0)
 
 
@@ -76,8 +76,8 @@
     g2, hl2, hr2, fl2, fr2, s2, t2,
     fp, hlf, hrf, flf, frf, sf, tf,
     ep, hle, hre, fle, fre, se, te,
-    m_all, r_all, eo, eg, reo, reg, so, sg, lo, ro, lg, rg, fo, fg, yo, yg, ryo, ryg,
-    send, recv,
+    m_all, p_all, r_all, eo, eg, reo, reg, so, sg, lo, ro, lg, rg, fo, fg, yo, yg, ryo, ryg,
+    send, recv, gates, own_sems,
 ):
     d = lax.axis_index("dp")
     m = lax.axis_index("mp")
@@ -98,6 +98,17 @@
     z_left = (d, h * 16 + lax.rem(z + 7, 8) * 2 + c)
     core_peer = (d, m + 1 - 2 * c)
 
+    loads = [
+        pltpu.make_async_copy(src, dst, own_sems.at[i])
+        for i, (src, dst) in enumerate(
+            (
+                (wo_ref, ow.at[:128]), (wout_ref, ow.at[128:]),
+                (wqkv_ref, bw.at[:, :384]), (win_ref, bw.at[:, 384:]),
+            )
+        )
+    ]
+    for load in loads:
+        load.start()
     barrier = pltpu.get_barrier_semaphore()
     everyone = x_peers + y_peers + [hi_peer, z_right, z_left, core_peer]
     for peer in everyone:
@@ -150,10 +161,6 @@
     local_centre = inputs - local_mean
     local_m2 = jnp.sum(local_centre * local_centre, 1, keepdims=True)
     stats[x, y] = columns_to_rows(local_mean, local_m2)
-    bw[:, :384] = wqkv_ref[...]
-    bw[:, 384:] = win_ref[...]
-    ow[:128] = wo_ref[...]
-    ow[128:] = wout_ref[...]
     pl.semaphore_wait(barrier, len(everyone))
 
     def hi_start(a):
@@ -304,6 +311,8 @@
     cg.own_step(4)
     cg.ready(0)
     cg.ready(1)
+    for load in loads:
+        load.wait()
     g_product(0)
     ng.other_step(2)
     ng.own_step(3)
@@ -433,9 +442,13 @@
         GELU_ROOT * (1.0 + 3.0 * GELU_CUBE * (pre * pre))
     )
     gs.send_y(2)
+    ms.along_y(1, ms.send_near)
+    ms.send_far(y)
     grad_mixed = gs.result()
     grad_attn = grad_mixed[:, :128].astype(BF16)
-    r_all[x, y, :, 384:] = (grad_mixed[:, 128:] * slope).astype(BF16)
+    p_all[x, y] = (grad_mixed[:, 128:] * slope).astype(BF16)
+    ps = Spread(p_all)
+    ps.send_near(y)
     dprob = mm_nt(grad_attn, value_b)
     delta = jnp.sum(prob * dprob, -1, keepdims=True)
     dscore = (prob * (dprob - delta)).astype(BF16)
@@ -443,19 +456,21 @@
     grad_kn = mm_tn(dscore, query_b) * FACTOR
     r_all[x, y, :, :128] = head_back(grad_qn, query_unit, query_scale, qg).astype(BF16)
     r_all[x, y, :, 128:256] = head_back(grad_kn, key_unit, key_scale, kg).astype(BF16)
-    r_all[x, y, :, 256:384] = mm_tn(prob_b, grad_attn).astype(BF16)
+    r_all[x, y, :, 256:] = mm_tn(prob_b, grad_attn).astype(BF16)
     rs = Spread(r_all)
     rs.send_near(y)
-    ms.along_y(1, ms.send_near)
-    ms.send_far(y)
-    rs.along_y(1)
     ms.along_y(2, ms.send_near)
     ms.far_step(1)
-    rs.along_y(2)
+    ps.along_y(1)
+    rs.along_y(1)
     ms.along_y(3, ms.send_near)
     ms.far_step(2)
+    ps.along_y(2)
+    rs.along_y(2)
+    ps.send_near(2, y != 2)
     rs.send_near(2, y != 2)
     ms.far_step(3)
+    ps.send_near(1, y != 1)
     rs.send_near(1, y != 1)
 
     class Reduce:
@@ -509,56 +524,74 @@
     grads = Reduce(eg, reg, sg, lg, rg, fg, yg, ryg)
 
     def grad_product(yy):
+        ps.ready(yy)
+        part = mm_nt(p_all[:, yy].reshape(512, 384), bw[:, 384:])
         rs.ready(yy)
-        grads.chunk(yy, mm_nt(r_all[:, yy].reshape(512, 768), bw[...]))
+        grads.chunk(yy, part + mm_nt(r_all[:, yy].reshape(512, 384), bw[:, :384]))
 
     def out_product(yy):
         ms.ready(yy)
         outs.chunk(yy, mm(m_all[:, yy].reshape(512, 512), ow[...]))
 
     out_product(2)
+    ps.along_y(3)
     rs.along_y(3)
+    ps.send_near(3, y != 3)
     rs.send_near(3, y != 3)
     out_product(1)
+    ps.send_far(2)
     rs.send_far(2)
+    ps.send_near(0, y != 0)
+    rs.send_near(0, y != 0)
     outs.core_sum(2)
     outs.step(1)
     out_product(3)
-    rs.send_near(0, y != 0)
     out_product(0)
+    ps.send_far(1)
     rs.send_far(1)
+    grad_product(2)
     outs.core_sum(1)
     outs.core_sum(3)
     outs.core_sum(0)
-    outs.step(2)
+    ps.send_far(3)
     rs.send_far(3)
-    grad_product(2)
-    rs.send_far(0)
     grads.core_sum(2)
     grads.step(1)
-    outs.step(3)
+    outs.step(2)
     grad_product(1)
+    ps.send_far(0)
+    rs.send_far(0)
     grads.core_sum(1)
     grads.step(2)
-    outs.step(4)
+    outs.step(3)
     grad_product(3)
     grads.core_sum(3)
     grads.step(3)
+    outs.step(4)
     grad_product(0)
     grads.core_sum(0)
     grads.step(4)
     outs.last()
-    weight = jnp.zeros((FEATURES, 768), F32)
-    for yy in range(4):
-        weight = weight + mm_tn(rows_of(nrm_all, yy), r_all[:, yy].reshape(512, 768))
-    gwqkv_ref[...] = weight[:, :384].astype(BF16)
-    gwin_ref[...] = weight[:, 384:].astype(BF16)
+    stores = []
+
+    def store(rows, value, target):
+        i = len(stores)
+        gates[rows] = value.astype(BF16)
+        copy = pltpu.make_async_copy(gates.at[rows], target, own_sems.at[4 + i])
+        copy.start()
+        stores.append(copy)
+
+    for i, (source, target) in enumerate(((r_all, gwqkv_ref), (p_all, gwin_ref))):
+        weight = jnp.zeros((FEATURES, 384), F32)
+        for yy in range(4):
+            weight = weight + mm_tn(rows_of(nrm_all, yy), source[:, yy].reshape(512, 384))
+        store(pl.ds(384 * i, 384), weight, target)
     grads.last()
     weight = jnp.zeros((512, FEATURES), F32)
     for yy in range(4):
         weight = weight + mm_tn(m_all[:, yy].reshape(512, 512), rows_of(cot_all, yy))
-    gwo_ref[...] = weight[:128].astype(BF16)
-    gwout_ref[...] = weight[128:].astype(BF16)
+    store(pl.ds(768, 128), weight[:128], gwo_ref)
+    store(pl.ds(896, 384), weight[128:], gwout_ref)
     out_ref[...] = (up(x_ref[...]) + outs.result()).astype(BF16)
     local_grad = grads.result() * gain
     centred = cen_ref[...]
@@ -574,6 +607,8 @@
     gx_ref[...] = (
         up(cot_ref[...]) + scaling * (local_grad - first - centred * second)
     ).astype(BF16)
+    for copy in stores:
+        copy.wait()
     for copy, when in started[-SENDS:]:
         finish(copy, when)
 
@@ -600,12 +635,13 @@
         pltpu.VMEM((4, 4, 8, 128), F32), pltpu.VMEM((4, 4, 8, 128), F32),
         pltpu.VMEM((64, 384), F32), pltpu.VMEM((64, 128), F32),
         *scatter(512), *scatter(384), *scatter(384),
-        vmem(4, 4, 128, 512), vmem(4, 4, 128, 768),
+        vmem(4, 4, 128, 512), vmem(4, 4, 128, 384), vmem(4, 4, 128, 384),
         vmem(4, 4, 2, 64, 384), vmem(4, 4, 2, 64, 384), vmem(4, 4, 64, 384), vmem(4, 4, 64, 384),
         vmem(8, 2, 64, 384), vmem(8, 2, 64, 384), ring, ring, ring, ring,
         pltpu.VMEM((2, 64, 384), F32), pltpu.VMEM((2, 64, 384), F32),
         vmem(64, 384), vmem(64, 384), vmem(64, 384), vmem(64, 384),
         pltpu.SemaphoreType.DMA((SENDS,)), pltpu.SemaphoreType.DMA((ARRIVALS,)),
+        vmem(1280, 384), pltpu.SemaphoreType.DMA((8,)),
     ]
     args = (block_input, cotangent, ln_gain, w_qkv, w_in, w_o, w_out, q_gain, k_gain)
     outs = (block_input, cotangent, w_qkv, w_in, w_o, w_out)
@@ -613,8 +649,10 @@
     results = pl.pallas_call(
         kernel,
         out_shape=shapes,
-        in_specs=[pl.BlockSpec(memory_space=pltpu.VMEM)] * len(args),
-        out_specs=tuple(pl.BlockSpec(memory_space=pltpu.VMEM) for _ in outs),
+        in_specs=[pl.BlockSpec(memory_space=pl.ANY if 3 <= i < 7 else pltpu.VMEM) for i in range(9)],
+        out_specs=tuple(
+            pl.BlockSpec(memory_space=pltpu.VMEM if i < 2 else pl.ANY) for i in range(6)
+        ),
         scratch_shapes=scratch,
         compiler_params=pltpu.CompilerParams(
             collective_id=1, has_side_effects=True, vmem_limit_bytes=56 * 2**20

time: 158 us -> 151 us (0.956)
  Pallas kernels: 156 us -> 150 us
    pallas_call x1, Pallas kernels: 154 us -> 147 us  [shards(): pl.pallas_call(kernel, out_shape=shapes, in_specs=[pl.BlockSpec(memory_sp...]
where the time goes in v4:
time: 151 us; the launch traced here: 150 us
  Pallas kernels  150 us (99%)
    pallas_call x1, Pallas kernels, shards(): pl.pallas_call(kernel, out_shape=shapes, in_specs=[pl.BlockSpec(memory_sp...  147 us

profile of v4, /device:TPU:6, one launch (start us, length us, event | category | flops | bytes accessed | tf_op | source)
XLA Modules:
  0.0 150.3 jit_solution(14691770316613212854)
XLA Ops:
  0.6 147.4 %block.1 = (bf16[64,384]{1,0:T(8,128)(2,1)}, bf16[64,384]{1,0:T(8,128)(2,1)}, bf16[384,384]{1,0:T(8,128)(2,1)}, bf16[384,384]{1,0:T(8,128)(2,1)}, bf16[128,384]{1,0:T(8,128)(2,1)}, /*index=5*/bf16[384,384]{1,0:T(8,128)(2,1)}) custom-call(bf16[64,384]{1,0:T(8,128)(2,1)} %x_ref.1, bf16[64,384]{1,0:T(8,128)(2,1)} %cot_ref.1, f32[384]{0:T(512)} %gain_ref.1, ...), custom_call_target="tpu_custom_call" | custom-call | tf_op jit(solution)/shard_map/block/pallas_call | solution.py:649
  148.0 2.2 %place.1 = (bf16[64,384]{1,0:T(8,128)(2,1)}, bf16[64,384]{1,0:T(8,128)(2,1)}, bf16[384,384]{1,0:T(8,128)(2,1)}, bf16[384,384]{1,0:T(8,128)(2,1)}, bf16[128,384]{1,0:T(8,128)(2,1)}, /*index=5*/bf16[384,384]{1,0:T(8,128)(2,1)}) custom-call(bf16[64,384]{1,0:T(8,128)(2,1)} %get-tuple-element.12.refs_0_, bf16[64,384]{1,0:T(8,128)(2,1)} %get-tuple-element.13.refs_1_, ...), custom_call_target="tpu_custom_call" | custom-call | tf_op jit(solution)/shard_map/place/pallas_call | solution.py:662
